TPU v7x, 512 devices: a whole 4x8x8 slice. The times are simulated.
512 devices in a mesh: dp: 128 (over y, z, core), mp: 4 (over x).
Axes of the slice: x: 4, y: 8, z: 8, core: 2. Of those that a mesh axis runs over, the one named last changes fastest.
Arguments:
- hidden: bfloat16 [3072, 4096], P('dp', 'mp')
- adapter_down_weight: bfloat16 [16, 4096], P(None, 'mp'), may hold values from -0.09375 to 0.09375
- adapter_up_weight: bfloat16 [16, 4096], P(None, 'mp'), may hold values from -1.5 to 1.5
- passages: bfloat16 [49152, 4096], P('dp', 'mp')
- candidate_passage_ids: int32 [3072, 8], P('dp'), may hold values from 0 to 49151, as said below
- storage: int32 [49152], replicated, may hold values from 0 to 49151, as said below
Outputs:
- mean_loss: float32 [], replicated
- grad_a: float32 [16, 4096], P(None, 'mp')
- grad_b: float32 [16, 4096], P(None, 'mp')
- grad_passages: bfloat16 [49152, 4096], P('dp', 'mp')
Inputs may be any that keep to these rules, and one draw needn't show every extreme that they name: `candidate_passage_ids`: passage ids. The storage row of every listed passage lies with dp index storage row // 384; among the 192 listed passages of each block of 24 queries, at most 3 lie with one dp index, and in every block some index holds exactly 3. Ids may repeat. A permutation: each storage row holds one passage.
All inputs are finite; a program needn't handle non-finite values.
Results may differ from a plain program's by a relative error of at most 0.0081.
Values may be sent and summed in bfloat16 or wider, within the bound.
A program may use at most 64 MiB of HBM per device.

v0:
```python
import math

import jax
import jax.numpy as jnp
from jax import lax
from jax.sharding import PartitionSpec as P

EMBED_WIDTH = 4096


SOFTMAX_TEMPER = 0.02
EPSILON = 1e-06


def contracted_rows(first_op, second_op):
    return lax.dot_general(
        first_op, second_op, (((1,), (1,)), ((), ())), preferred_element_type=jnp.float32
    )


def contract_cols(first_op, second_op):
    return lax.dot_general(
        first_op, second_op, (((0,), (0,)), ((), ())), preferred_element_type=jnp.float32
    )


def lookup_rows(source_table, indices):
    return jnp.take(source_table, indices, axis=0, mode="fill", fill_value=0)


def send_rows(found_rows):
    return lax.all_to_all(found_rows, "dp", split_axis=0, concat_axis=0, tiled=True)


def softmax_terms(scores, positive_cols, logit_scale):
    row_max = jnp.max(scores, axis=1, keepdims=True)
    exponent = jnp.exp(scores - row_max)
    totals = jnp.sum(exponent, axis=1, keepdims=True)
    columns = lax.broadcasted_iota(jnp.int32, scores.shape, 1)
    picked = (columns == positive_cols[:, None]).astype(jnp.float32)
    loss_rows = jnp.log(totals[:, 0]) + row_max[:, 0] - jnp.sum(scores * picked, axis=1)
    weights = ((exponent / totals - picked) * logit_scale).astype(jnp.bfloat16)
    return (weights, loss_rows)


def shards(
    hidden, adapter_down_weight, adapter_up_weight, passages, candidate_passage_ids, storage
):
    data_count = lax.axis_size("dp")
    model_shard_count = lax.axis_size("mp")
    query_rows, feature_columns = hidden.shape
    listed = candidate_passage_ids.shape[1]
    resident = passages.shape[0]
    block_rows = query_rows * listed
    capacity = 2 * block_rows // data_count
    logit_scale = 1.0 / (SOFTMAX_TEMPER * math.sqrt(feature_columns * model_shard_count))
    hidden_full_width = hidden.astype(jnp.float32)
    partial_reduced = contracted_rows(hidden, adapter_down_weight)
    low_rank = lax.psum(partial_reduced, "mp")
    reduced_projection = low_rank.astype(jnp.bfloat16)
    combined_rows = hidden_full_width + jnp.dot(
        reduced_projection, adapter_up_weight, preferred_element_type=jnp.float32
    )
    sum_squares = lax.psum(jnp.sum(combined_rows * combined_rows, axis=1), "mp")
    inverse_norm = lax.rsqrt(sum_squares[:, None] / EMBED_WIDTH + EPSILON)
    query_wide = combined_rows * inverse_norm
    query_half = query_wide.astype(jnp.bfloat16)
    located = jnp.take(storage, candidate_passage_ids.reshape(-1), axis=0)
    owners = located // resident
    local_rows = located - owners * resident
    owner_hits = (owners[:, None] == jnp.arange(data_count, dtype=jnp.int32)[None, :]).astype(
        jnp.int32
    )
    slot_index = jnp.sum((jnp.cumsum(owner_hits, axis=0) - owner_hits) * owner_hits, axis=1)
    wanted = (
        jnp.full((data_count, capacity), resident, jnp.int32).at[owners, slot_index].set(local_rows)
    )
    served = lax.all_to_all(wanted, "dp", split_axis=0, concat_axis=0, tiled=True)
    returned = send_rows(lookup_rows(passages, served))
    candidates = returned[owners, slot_index]
    partial_scores = contracted_rows(query_half, candidates)
    scores = lax.psum(partial_scores, "mp") * logit_scale
    positive_cols = jnp.arange(query_rows, dtype=jnp.int32) * listed
    weights, loss_rows = softmax_terms(scores, positive_cols, logit_scale)
    query_grad = jnp.dot(weights, candidates, preferred_element_type=jnp.float32)
    cand_grad = contract_cols(weights, query_half).astype(jnp.bfloat16)
    outgoing = (
        jnp.zeros((data_count, capacity, feature_columns), jnp.bfloat16)
        .at[owners, slot_index]
        .set(cand_grad)
    )
    incoming = lax.all_to_all(outgoing, "dp", split_axis=0, concat_axis=0, tiled=True)
    table_grad = (
        jnp.zeros((resident, feature_columns), jnp.float32)
        .at[served.reshape(-1)]
        .add(incoming.reshape(-1, feature_columns).astype(jnp.float32), mode="drop")
    )
    tangent = lax.psum(jnp.sum(query_wide * query_grad, axis=1), "mp")
    combined_gradient = (
        inverse_norm * (query_grad - query_wide * (tangent[:, None] / EMBED_WIDTH))
    ).astype(jnp.bfloat16)
    grad_b_part = contract_cols(reduced_projection, combined_gradient)
    reduced_gradient = lax.psum(contracted_rows(combined_gradient, adapter_up_weight), "mp").astype(
        jnp.bfloat16
    )
    grad_a_part = contract_cols(reduced_gradient, hidden)
    grad_a, grad_b, loss_total = lax.psum((grad_a_part, grad_b_part, jnp.sum(loss_rows)), "dp")
    mean_loss = loss_total / (query_rows * data_count)
    return (mean_loss, grad_a, grad_b, table_grad.astype(jnp.bfloat16))


def solution(mesh):
    return jax.shard_map(
        shards,
        mesh=mesh,
        in_specs=(P("dp", "mp"), P(None, "mp"), P(None, "mp"), P("dp", "mp"), P("dp", None), P()),
        out_specs=(P(), P(None, "mp"), P(None, "mp"), P("dp", "mp")),
        check_vma=False,
    )
```

profile of v0, /device:TPU:1, one launch (start us, length us, event | category | flops | bytes accessed | tf_op | source)
XLA Modules:
  0.0 421.9 jit_solution(1274007915167908873)
XLA Ops:
  7.2 0.8 copy.19
  8.2 2.2 gather_fusion
  11.0 9.3 %scatter_fusion = s32[128,3]{0,1:T(4,128)S(1)} fusion(s32[128,3]{0,1:T(4,128)S(1)} %broadcast_in_dim.24, s32[192]{0:T(256)S(1)} %bitcast.37, s32[192]{0:T(256)S(1)} %get-tuple-element.8), kind=kCustom, calls=%fused_computation.3 | custom fusion | bytes 3840 | tf_op jit(solution)/shard_map/scatter | solution.py:76
  20.4 29.7 %all_to_all.25 = s32[128,1,3]{2,1,0:T(1,128)S(1)} all-to-all(s32[128,1,3]{2,1,0:T(1,128)S(1)} %copy.23), channel_id=1, replica_groups=mesh['dp'=128,'mp'=4] {'dp'}, dimensions={0} | all-to-all | bytes 3072 | tf_op jit(solution)/shard_map/all_to_all | solution.py:78
  50.5 2.1 gather_fusion.1
  53.6 1.7 copy.26
  55.3 5.7 %all-to-all-start.1 = ((bf16[128,3,1024]{2,1,0:T(4,128)(2,1)}), bf16[128,3,1024]{2,1,0:T(4,128)(2,1)S(1)}, u32[]{:S(2)}, u32[]{:S(2)}) async-start(bf16[128,3,1024]{2,1,0:T(4,128)(2,1)} %copy.26), calls=%async_computation.1 | async-start | bytes 2097152 | tf_op jit(solution)/shard_map/all_to_all | solution.py:32
  61.2 9.1 %psum.56 = bf16[24,16]{0,1:T(8,128)(2,1)S(1)} all-reduce(f32[24,16]{0,1:T(8,128)S(1)} %fusion.17), channel_id=1, replica_groups=mesh['dp'=128,'mp'=4] {'mp'}, use_global_device_ids=true, to_apply=%region_0.0 | all-reduce | flops 384 | bytes 2304 | tf_op jit(solution)/shard_map/psum | solution.py:59
  70.6 6.8 %psum.57 = f32[24]{0:T(128)S(1)} all-reduce(f32[24]{0:T(128)S(1)} %get-tuple-element.12), channel_id=1, replica_groups=mesh['dp'=128,'mp'=4] {'mp'}, use_global_device_ids=true, to_apply=%region_2.0 | all-reduce | flops 24 | bytes 192 | tf_op jit(solution)/shard_map/psum | solution.py:64
  77.9 0.8 reduce.5
  78.9 12.5 %all-to-all-done.1 = bf16[128,3,1024]{2,1,0:T(4,128)(2,1)S(1)} async-done(((bf16[128,3,1024]{2,1,0:T(4,128)(2,1)}), bf16[128,3,1024]{2,1,0:T(4,128)(2,1)S(1)}, u32[]{:S(2)}, u32[]{:S(2)}) %all-to-all-start.1) | async-done | bytes 786464 | tf_op jit(solution)/shard_map/all_to_all | solution.py:32
  91.7 3.2 gather_fusion.2
  95.2 13.3 %psum.58 = f32[24,192]{1,0:T(8,128)S(1)} all-reduce(f32[24,192]{1,0:T(8,128)S(1)} %fusion.14), channel_id=1, replica_groups=mesh['dp'=128,'mp'=4] {'mp'}, use_global_device_ids=true, to_apply=%region_7.8 | all-reduce | flops 4608 | bytes 36864 | tf_op jit(solution)/shard_map/psum | solution.py:82
  109.2 12.7 %scatter_fusion.1 = bf16[128,3,1024]{2,0,1:T(8,128)(2,1)S(1)} fusion(bf16[128,3,1024]{2,0,1:T(8,128)(2,1)S(1)} %broadcast_in_dim.46, s32[192]{0:T(256)S(1)} %bitcast.38, bf16[192,1024]{1,0:T(8,128)(2,1)S(1)} %convolution_convert_fusion), kind=kCustom, calls=%fused_computation.4 | custom fusion | bytes 1181184 | tf_op jit(solution)/shard_map/scatter | solution.py:90
  122.0 1.7 copy.28
  123.7 10.8 %all-to-all-start.2 = ((bf16[128,3,1024]{2,1,0:T(4,128)(2,1)}), bf16[128,3,1024]{2,1,0:T(4,128)(2,1)S(1)}, u32[]{:S(2)}, u32[]{:S(2)}) async-start(bf16[128,3,1024]{2,1,0:T(4,128)(2,1)} %copy.28), calls=%async_computation.2 | async-start | bytes 2097152 | tf_op jit(solution)/shard_map/all_to_all | solution.py:92
  134.9 6.6 %psum.60 = f32[24]{0:T(128)S(1)} all-reduce(f32[24]{0:T(128)S(1)} %get-tuple-element.14), channel_id=1, replica_groups=mesh['dp'=128,'mp'=4] {'mp'}, use_global_device_ids=true, to_apply=%region_14.15 | all-reduce | flops 24 | bytes 192 | tf_op jit(solution)/shard_map/psum | solution.py:98
  141.7 8.1 %psum.61 = bf16[24,16]{0,1:T(8,128)(2,1)S(1)} all-reduce(f32[24,16]{0,1:T(8,128)S(1)} %fusion.18), channel_id=1, replica_groups=mesh['dp'=128,'mp'=4] {'mp'}, use_global_device_ids=true, to_apply=%region_15.16 | all-reduce | flops 384 | bytes 2304 | tf_op jit(solution)/shard_map/psum | solution.py:103
  152.0 250.9 %psum.59 = f32[]{:T(128)} all-reduce(f32[]{:T(128)} %subtract_reduce_fusion), channel_id=1, replica_groups=mesh['dp'=128,'mp'=4] {'dp'}, use_global_device_ids=true, to_apply=%region_12.13 | all-reduce | flops 1 | bytes 8 | tf_op jit(solution)/shard_map/psum | solution.py:107
  403.6 1.5 reshape.267
  405.1 4.9 %scatter_custom_fusion.2 = f32[384,1024]{1,0:T(8,128)S(1)} fusion(s32[384]{0:T(512)S(1)} %fusion.12, f32[384,1024]{1,0:T(8,128)} %reshape.267, f32[]{:T(128)} %constant.30.clone.1), kind=kCustom, calls=%fused_computation.9 | custom fusion | flops 393216 | bytes 1573376 | tf_op jit(solution)/shard_map/scatter-add | solution.py:96
  410.0 1.0 convert_element_type.48
  411.0 1.5 copy.36
  412.4 1.5 copy.37
  (57 shorter events, 7.4 us)
Async XLA Ops:
  7.2 43.3 %copy-start = (bf16[384,1024]{1,0:T(8,128)(2,1)S(1)}, bf16[384,1024]{1,0:T(8,128)(2,1)}, u32[]{:S(2)}) copy-start(bf16[384,1024]{1,0:T(8,128)(2,1)} %param.9) | copy-start | bytes 2359300
  53.6 7.4 %copy-start.1 = (bf16[24,1024]{1,0:T(8,128)(2,1)S(1)}, bf16[24,1024]{1,0:T(8,128)(2,1)}, u32[]{:S(2)}) copy-start(bf16[24,1024]{1,0:T(8,128)(2,1)} %param.6) | copy-start | bytes 147460
  53.6 7.4 %copy-start.3 = (bf16[16,1024]{1,0:T(8,128)(2,1)S(1)}, bf16[16,1024]{1,0:T(8,128)(2,1)}, u32[]{:S(2)}) copy-start(bf16[16,1024]{1,0:T(8,128)(2,1)} %param.7) | copy-start | bytes 98308
  53.6 16.7 %copy-start.2 = (bf16[16,1024]{1,0:T(8,128)(2,1)S(1)}, bf16[16,1024]{1,0:T(8,128)(2,1)}, u32[]{:S(2)}) copy-start(bf16[16,1024]{1,0:T(8,128)(2,1)} %param.8) | copy-start | bytes 98308
  55.3 36.1 %all-to-all-start.1 = ((bf16[128,3,1024]{2,1,0:T(4,128)(2,1)}), bf16[128,3,1024]{2,1,0:T(4,128)(2,1)S(1)}, u32[]{:S(2)}, u32[]{:S(2)}) async-start(bf16[128,3,1024]{2,1,0:T(4,128)(2,1)} %copy.26), calls=%async_computation.1 | async-start | bytes 2097152 | tf_op jit(solution)/shard_map/all_to_all | solution.py:32
  123.7 279.9 %all-to-all-start.2 = ((bf16[128,3,1024]{2,1,0:T(4,128)(2,1)}), bf16[128,3,1024]{2,1,0:T(4,128)(2,1)S(1)}, u32[]{:S(2)}, u32[]{:S(2)}) async-start(bf16[128,3,1024]{2,1,0:T(4,128)(2,1)} %copy.28), calls=%async_computation.2 | async-start | bytes 2097152 | tf_op jit(solution)/shard_map/all_to_all | solution.py:92
  134.5 276.5 %all-reduce.4.cloned.1.call-start = ((), (), s32[]{:S(2)}) async-start(), calls=%async_computation.3 | async-start | bytes 262144 | tf_op jit(solution)/shard_map/psum | solution.py:107
Sparse Core Ops, SparseCore 0:
  151.5 184.5 all-reduce.3
where the time goes:
time: 422 us
  blocking collectives  325 us (77%)
  local copies, waits for them, and re-layouts  40.3 us (10%)
  starting transfers between devices  16.6 us (4%)
  between operations  16.1 us (4%)
  waiting for transfers between devices  12.5 us (3%)
  other arithmetic  8.81 us (2%)
    psum x1, blocking collectives, shards(): lax.psum((grad_a_part, grad_b_part, jnp.sum(loss_rows)), 'dp')  251 us
    all_to_all x1, blocking collectives, shards(): lax.all_to_all(wanted, 'dp', split_axis=0, concat_axis=0, tiled=True)  29.7 us
    scatter x2, local copies, waits for them, and re-layouts, shards(): outgoing = jnp.zeros((data_count, capacity, feature_columns), jnp.bfloat1...  14.4 us
    psum x1, blocking collectives, shards(): scores = lax.psum(partial_scores, 'mp') * logit_scale  13.3 us
    all_to_all x1, waiting for transfers between devices, send_rows(): lax.all_to_all(found_rows, 'dp', split_axis=0, concat_axis=0, tiled=True)  12.5 us
    all_to_all x1, starting transfers between devices, shards(): lax.all_to_all(outgoing, 'dp', split_axis=0, concat_axis=0, tiled=True)  10.8 us
    scatter x1, local copies, waits for them, and re-layouts, shards(): jnp.full((data_count, capacity), resident, jnp.int32).at[owners, slot_index]  9.28 us
    psum x1, blocking collectives, shards(): low_rank = lax.psum(partial_reduced, 'mp')  9.14 us
  transfers between devices with their start and end apart: 3, of which 1 were waited for; matrix products, arithmetic and copies ran while one was open for 3% of the time, Pallas kernels for 0%

commit v1 on v0

v1 whole, which is shorter than its diff:
```python
import functools
import math

import jax
import jax.numpy as jnp
from jax import lax
from jax.experimental import pallas as pl
from jax.experimental.pallas import tpu as pltpu
from jax.sharding import PartitionSpec as P

SOFTMAX_TEMPER = 0.02
EPSILON = 1e-06
MESH = pl.DeviceIdType.MESH
F32, BF16 = jnp.float32, jnp.bfloat16
SLOTS = 3
NY = NZ = 8
NX = 4
Q = 24
LISTED = 8
CHIP = 2 * Q
RANK = 16
ROWS = 384
WIDTH = 1024
HALF = WIDTH // 2
DEVS = 2 * NY * NZ
GROUP = NZ * CHIP
VOFF = SLOTS * Q
G_LANE, LOSS_LANE = 120, 121
TINY = 2.0**-80
NEG = -1e38


def nn(a, b):
    return lax.dot_general(a, b, (((1,), (0,)), ((), ())), preferred_element_type=F32)


def nt(a, b):
    return lax.dot_general(a, b, (((1,), (1,)), ((), ())), preferred_element_type=F32)


def tn(a, b):
    return lax.dot_general(a, b, (((0,), (0,)), ((), ())), preferred_element_type=F32)


def exact(dims, a, b):
    return lax.dot_general(a, b, (dims, ((), ())), preferred_element_type=F32, precision=lax.Precision.HIGHEST)


def split(x, parts):
    out = []
    for _ in range(parts):
        top = x.astype(BF16)
        out.append(top)
        x = x - top.astype(F32)
    return out


def iota(shape, dim):
    return lax.broadcasted_iota(jnp.int32, shape, dim)


def kernel(
    ids_ref, hidden_ref, down_ref, up_ref, pass_ref, storage_ref,
    loss_ref, ga_ref, gb_ref, table_ref,
    hbuf, mine, theirs, xb1, xb2, locs, lists, pick, picked, folds, diag, rsx, part, summed, got, back, wrec,
    cand, piece_out, piece_in, piece_sum, final, mixed_ref,
    st_sem, e1_sem, e2_sem, l_sem, lz_sem, ly_sem, ring_sem, sib_sem, rsx_sem, got_sem, w_sem, rs_sem, ag_sem,
    send_sem, small_sem,
):
    me, mp = lax.axis_index("dp"), lax.axis_index("mp")
    core, chip_me = lax.rem(me, 2), me // 2
    y, z = chip_me // NZ, lax.rem(chip_me, NZ)

    def dev(yy, zz, c):
        return ((lax.rem(yy + NY, NY) * NZ + lax.rem(zz + NZ, NZ)) * 2 + c, mp)

    def push(src, dst, ssem, rsem, target):
        pltpu.make_async_remote_copy(
            src_ref=src, dst_ref=dst, send_sem=ssem, recv_sem=rsem, device_id=target, device_id_type=MESH
        ).start()

    def take(ref, sem):
        pltpu.make_async_copy(ref, ref, sem).wait()

    sibling = (chip_me * 2 + 1 - core, mp)

    bar = pltpu.get_barrier_semaphore()
    for t in (dev(y + 1, z, core), dev(y - 1, z, core), dev(y, z + 1, core), dev(y, z - 1, core), sibling):
        pl.semaphore_signal(bar, inc=1, device_id=t, device_id_type=MESH)
    for i in range(1, NX):
        pl.semaphore_signal(bar, inc=1, device_id=(me, lax.rem(mp + i, NX)), device_id_type=MESH)

    hid32 = hidden_ref[...].astype(F32)
    up32 = up_ref[...].astype(F32)
    mine[...] = jnp.concatenate([hid32, jnp.zeros((8, WIDTH), F32)], axis=0).astype(BF16)
    left = jnp.concatenate([hid32, up32], axis=0).astype(BF16)
    right = jnp.concatenate([down_ref[...].astype(F32), up32, jnp.zeros((96, WIDTH), F32)], axis=0).astype(BF16)
    prod = nt(left, right)
    biggest = jnp.max(jnp.max(jnp.abs(pass_ref[...].astype(F32)), axis=0, keepdims=True), axis=1, keepdims=True)
    lane40, row40 = iota((40, 128), 1), iota((40, 128), 0)
    xb1[mp] = jnp.where((lane40 == 40) & (row40 == 0), biggest, prod)

    pl.semaphore_wait(bar, 5 + NX - 1)
    push(mine, theirs, small_sem.at[0], st_sem, sibling)
    for i in range(1, NX):
        push(xb1.at[mp], xb1.at[mp], small_sem.at[1], e1_sem, (me, lax.rem(mp + i, NX)))

    lane1 = iota((1, 128), 1)
    for j in range(Q * LISTED):
        pid = ids_ref[j // LISTED, j % LISTED]
        row = storage_ref[pl.ds(pid // 128, 1), :]
        locs[pl.ds(j, 1), :] = jnp.where(lane1 == lax.rem(pid, 128), row, 0).astype(F32)
    located = jnp.sum(locs[...], axis=1, keepdims=True)
    located = jnp.concatenate([located, jnp.full((64, 1), 1e6, F32)], axis=0)
    r256, l256 = iota((256, 256), 0), iota((256, 256), 1)
    as_row = jnp.sum(jnp.where(r256 == l256, located, 0.0), axis=0, keepdims=True)
    lists[0, pl.ds(me, 1), :] = as_row[:, 0:128]
    lists[1, pl.ds(me, 1), :] = as_row[:, 128:256]
    push(lists.at[:, pl.ds(me, 1), :], lists.at[:, pl.ds(me, 1), :], small_sem.at[2], l_sem, sibling)

    take(theirs, st_sem)
    theirs32 = theirs[0:Q, :].astype(F32)
    both = jnp.where(core == 0, jnp.concatenate([hid32, theirs32], axis=0), jnp.concatenate([theirs32, hid32], axis=0))
    hbuf[pl.ds(pl.multiple_of(chip_me * CHIP, 16), CHIP), :] = both.astype(BF16)

    sa, sb = NZ - (NZ - 1) * core, 1 + (NZ - 1) * core
    a = jnp.where(core == 0, y, z)
    b = jnp.where(core == 0, z, y)
    lanes = pl.ds(pl.multiple_of(core * HALF, HALF), HALF)

    def chip_of(aa, bb):
        return lax.rem(aa + 2 * NY, NY) * sa + lax.rem(bb + 2 * NY, NY) * sb

    def region(ci):
        return hbuf.at[pl.ds(pl.multiple_of(ci * CHIP, 16), CHIP), lanes]

    def pass_on(ci, target, rsem):
        push(region(ci), region(ci), send_sem, rsem, target)

    ar, al = (chip_of(a + 1, b) * 2 + core, mp), (chip_of(a - 1, b) * 2 + core, mp)
    br, bl = (chip_of(a, b + 1) * 2 + core, mp), (chip_of(a, b - 1) * 2 + core, mp)
    order = [0, -1, 1, -2, 2, -3, 3, -4]

    def steps(j, d):
        return 4 if (j % 2 == 0) == (d > 0) else 3

    def event(j, t):
        off = order[j]
        if t == 0:
            ci = chip_of(a + off, b)
            if j > 0:
                take(region(ci), ring_sem.at[ci])
            if j == 0 or (off < 0 and off > -4):
                pass_on(ci, ar, ring_sem.at[ci])
            if j == 0 or (off > 0 and off < 3):
                pass_on(ci, al, ring_sem.at[ci])
            pass_on(ci, br, ring_sem.at[ci])
            pass_on(ci, bl, ring_sem.at[ci])
            if j > 0:
                pass_on(ci, sibling, sib_sem.at[ci])
        else:
            for d in (1, -1):
                if t <= steps(j, d):
                    ci = chip_of(a + off, b - d * t)
                    take(region(ci), ring_sem.at[ci])
                    if t < steps(j, d):
                        pass_on(ci, br if d > 0 else bl, ring_sem.at[ci])
                    pass_on(ci, sibling, sib_sem.at[ci])

    event(0, 0)

    take(xb1.at[pl.ds(0, NX - 1)], e1_sem)
    tot = xb1[0] + xb1[1] + xb1[2] + xb1[3]
    most = jnp.maximum(jnp.maximum(xb1[0], xb1[1]), jnp.maximum(xb1[2], xb1[3]))
    most = jnp.max(jnp.where((lane40 == 40) & (row40 == 0), most, 0.0))
    shrink = jnp.where(most > 2.0**40, TINY, 1.0)
    low_half = tot[0:Q, 0:RANK].astype(BF16)
    rolled = pltpu.roll(tot, 128 - RANK, 1)
    hid_up, gram = rolled[0:Q, 0:RANK], rolled[Q : Q + RANK, 0:RANK]
    mixed = hid32 + nn(low_half, up_ref[...])
    mixed_ref[...] = mixed
    xb2[mp] = jnp.broadcast_to(jnp.sum(mixed * mixed, axis=1, keepdims=True), (Q, 128))
    for i in range(1, NX):
        push(xb2.at[mp], xb2.at[mp], small_sem.at[3], e2_sem, (me, lax.rem(mp + i, NX)))

    take(lists.at[:, pl.ds(0, 1), :], l_sem)

    def line(ref_rows, n):
        return lists.at[:, pl.ds(ref_rows, n), :]

    zr, zl = dev(y, z + 1, core), dev(y, z - 1, core)
    yr, yl = dev(y + 1, z, core), dev(y - 1, z, core)

    def list_step(t):
        if t <= 4:
            for d, to in ((1, zr), (-1, zl)):
                lim = 4 if d > 0 else 3
                if t > lim:
                    continue
                zz = lax.rem(z - d * t + 2 * NZ, NZ)
                rows = pl.multiple_of((y * NZ + zz) * 2, 2)
                if t > 0:
                    take(line(rows, 2), lz_sem.at[zz])
                if t < lim:
                    push(line(rows, 2), line(rows, 2), small_sem.at[4], lz_sem.at[zz], to)
        if t >= 4:
            u = t - 4
            for d, to in ((1, yr), (-1, yl)):
                lim = 4 if d > 0 else 3
                if u > lim:
                    continue
                yy = lax.rem(y - d * u + 2 * NY, NY)
                rows = pl.multiple_of(yy * 2 * NZ, 2 * NZ)
                if u > 0:
                    take(line(rows, 2 * NZ), ly_sem.at[yy])
                if u < lim:
                    push(line(rows, 2 * NZ), line(rows, 2 * NZ), small_sem.at[5], ly_sem.at[yy], to)

    list_step(0)

    events = sorted((j + 2 * t, t, j) for j in range(8) for t in range(5) if j + t > 0)
    sections = {}
    for n, (key, t, j) in enumerate(events):
        event(j, t)
        if n % 4 == 3 and n // 4 + 1 <= 8:
            list_step(n // 4 + 1)

    take(xb2.at[pl.ds(0, NX - 1)], e2_sem)
    inv_norm = lax.rsqrt((xb2[0] + xb2[1] + xb2[2] + xb2[3]) / (WIDTH * NX) + EPSILON)

    wanted = jnp.concatenate([lists[0], lists[1]], axis=1) - (me * ROWS).astype(F32)
    here = (wanted >= 0.0) & (wanted < ROWS)
    earlier = nn(here.astype(F32).astype(BF16), (r256 < l256).astype(F32).astype(BF16))
    rows_iota = iota((DEVS, ROWS), 1).astype(F32)
    group_mask = (iota((SLOTS * 16, GROUP), 1) // Q) == lax.rem(iota((SLOTS * 16, GROUP), 0), 16)
    part_pu = jnp.zeros((DEVS, 128), F32)
    for s in range(SLOTS):
        col = jnp.sum(jnp.where(here & (earlier == s), wanted + 1.0, 0.0), axis=1, keepdims=True) - 1.0
        pk = (rows_iota == col).astype(F32).astype(BF16)
        pick[s] = pk
        picked[s] = (nn(pk, pass_ref[...]) * shrink).astype(BF16)
        f_lane = iota((GROUP, 128), 1) - s * Q
        folds[s] = ((f_lane == lax.rem(iota((GROUP, 128), 0), Q)) & (f_lane >= 0)).astype(F32).astype(BF16)
        up_at = jnp.concatenate(
            [jnp.zeros((VOFF + s * RANK, WIDTH), F32), up32, jnp.zeros((128 - VOFF - (s + 1) * RANK, WIDTH), F32)], axis=0
        ).astype(BF16)
        part_pu = part_pu + nt(picked[s], up_at)

    owner = jnp.floor((located + 0.5) * (1.0 / ROWS))
    hold = (iota((256, 128), 1).astype(F32) == owner).astype(F32)
    hold_b = hold.astype(BF16)
    rank = jnp.sum(hold * nn((r256 > l256).astype(F32).astype(BF16), hold_b), axis=1, keepdims=True)
    count = tn(hold_b, jnp.ones((256, 128), BF16))
    l_col = iota((256, 128), 1)
    pos_at = (iota((256, 128), 0) == LISTED * lax.rem(l_col, Q)) & (rank == (l_col // Q).astype(F32)) & (l_col < VOFF)
    positive = tn(hold_b, pos_at.astype(F32).astype(BF16))
    lane = iota((DEVS, 128), 1)
    valid = (count > (lane // Q).astype(F32)) & (lane < VOFF)

    row128 = iota((128, RANK), 0)
    at_rank = ((row128 >= VOFF) & (row128 < VOFF + SLOTS * RANK) & (lax.rem(row128 - VOFF + 128 * RANK, RANK) == iota((128, RANK), 1)))
    at_rank = at_rank.astype(F32)
    at_query = ((iota((Q, 128), 1) < VOFF) & (lax.rem(iota((Q, 128), 1), Q) == iota((Q, 128), 0))).astype(F32)
    spread = nn(nt(at_rank.astype(BF16), low_half).astype(BF16), at_query.astype(BF16))
    row_a, lane_a = iota((128, 128), 0), iota((128, 128), 1)
    same_slot = ((row_a + 128 * RANK - VOFF) // RANK - 128) == lane_a // Q
    spread = jnp.where(same_slot, spread, 0.0).astype(BF16)
    inv_lane = jnp.sum(inv_norm * at_query, axis=0, keepdims=True)

    def rest(i, c):
        @pl.when(i != chip_me)
        def _():
            r = hbuf.at[pl.ds(pl.multiple_of(i * CHIP, 16), CHIP), pl.ds(pl.multiple_of(HALF - core * HALF, HALF), HALF)]
            take(r, sib_sem.at[i])
        return c

    lax.fori_loop(0, NY * NZ, rest, 0)

    def score(g, c):
        rows = pl.ds(pl.multiple_of(g * 16, 16), 16)
        s_g = jnp.concatenate([picked[s, rows, :] for s in range(SLOTS)], axis=0)
        d = nt(s_g, hbuf[pl.ds(pl.multiple_of(g * GROUP, 16), GROUP), :])
        d = jnp.where(group_mask, d, 0.0)
        acc = jnp.zeros((16, 128), F32)
        for s in range(SLOTS):
            for piece in split(d[s * 16 : (s + 1) * 16, :], 3):
                acc = acc + nn(piece, folds[s])
        part[rows, :] = acc
        return c

    lax.fori_loop(0, NY, score, 0)
    part[...] = part[...] + part_pu + jnp.where(lane == G_LANE, shrink * (1.0 / NX), 0.0)

    quarter = DEVS // NX

    def q_rows(k):
        return part.at[pl.ds(pl.multiple_of(k * quarter, quarter), quarter), :]

    for i in range(1, NX):
        k = lax.rem(mp + i, NX)
        push(q_rows(k), rsx.at[mp], small_sem.at[6], rsx_sem, (me, k))
    rsx[mp] = part[pl.ds(pl.multiple_of(mp * quarter, quarter), quarter), :]
    take(rsx.at[pl.ds(0, NX - 1)], rsx_sem)
    summed[...] = rsx[0] + rsx[1] + rsx[2] + rsx[3]

    def give(i, c):
        j = lax.rem(i + me, quarter)
        block = mp * quarter + j
        for dk in range(NX):
            k = lax.rem(mp + dk, NX)
            src = summed.at[pl.ds(j, 1), :]
            if dk == 0:
                @pl.when(block == me)
                def _():
                    pltpu.make_async_copy(src, got.at[pl.ds(me, 1), :], got_sem).start()

                @pl.when(block != me)
                def _():
                    push(src, got.at[pl.ds(me, 1), :], small_sem.at[7], got_sem, (block, k))
            else:
                push(src, got.at[pl.ds(me, 1), :], small_sem.at[7], got_sem, (block, k))
        return c

    lax.fori_loop(0, quarter, give, 0)
    take(got, got_sem)

    g = got[...]
    unshrink = jnp.sum(jnp.where(lane == G_LANE, g, 0.0), axis=1, keepdims=True)
    unshrink = jnp.where(unshrink < 0.5, 1.0 / TINY, 1.0)
    ranks = jnp.where((lane >= VOFF) & (lane < VOFF + SLOTS * RANK), g, 0.0)
    raw = g
    for piece in split(ranks, 3):
        raw = raw + nn(piece, spread)
    raw = jnp.where(valid & (inv_lane > 0.0), raw * inv_lane * unshrink, 0.0)
    scale = 1.0 / (SOFTMAX_TEMPER * math.sqrt(WIDTH * NX))
    scores = jnp.where(valid, raw * scale, NEG)

    def over_slots(x, op, fill):
        x0 = op(op(x, pltpu.roll(x, 128 - Q, 1)), pltpu.roll(x, 128 - 2 * Q, 1))
        return jnp.where(lane1 < Q, x0, jnp.where(lane1 < 2 * Q, pltpu.roll(x0, Q, 1), jnp.where(lane1 < 3 * Q, pltpu.roll(x0, 2 * Q, 1), fill)))

    top = over_slots(jnp.max(scores, axis=0, keepdims=True), jnp.maximum, 0.0)
    expo = jnp.where(valid, jnp.exp(scores - top), 0.0)
    total = over_slots(jnp.sum(expo, axis=0, keepdims=True), jnp.add, 1.0)
    own = over_slots(jnp.sum(jnp.where(positive > 0.5, scores, 0.0), axis=0, keepdims=True), jnp.add, 0.0)
    loss = jnp.sum(jnp.where(lane1 < Q, jnp.log(total) + top - own, 0.0), axis=1, keepdims=True)
    weights = jnp.where(valid, (expo / total - positive) * scale, 0.0)
    tangent = over_slots(jnp.sum(weights * raw, axis=0, keepdims=True), jnp.add, 0.0) / (WIDTH * NX)
    w2 = weights * inv_lane
    v = jnp.zeros((DEVS, 128), F32)
    for piece in split(w2, 3):
        v = v + nt(piece, spread)
    back[...] = w2 + v + jnp.where(lane == LOSS_LANE, loss, 0.0)

    def hand(i, c):
        t = lax.rem(me + 1 + i, DEVS)
        push(back.at[pl.ds(t, 1), :], wrec.at[pl.ds(me, 1), :], small_sem.at[8], w_sem, (t, mp))
        return c

    lax.fori_loop(0, DEVS - 1, hand, 0)
    pltpu.make_async_copy(back.at[pl.ds(me, 1), :], wrec.at[pl.ds(me, 1), :], w_sem).start()

    z_all = exact(((0,), (0,)), weights, ranks * unshrink)
    z_all = jnp.where(lane_a >= VOFF, z_all, 0.0)
    same_t = ((lane_a + 128 * RANK - VOFF) // RANK - 128) == row_a // Q
    z_all = jnp.where(same_t, z_all, 0.0)
    w_pu = exact(((1,), (0,)), exact(((1,), (0,)), at_query, z_all), at_rank)
    inv_col = inv_norm[:, 0:1]
    q_up = inv_col * (hid_up + exact(((1,), (0,)), low_half.astype(F32), gram))
    tan_col = jnp.sum(jnp.where((iota((Q, 128), 1) < Q), at_query, 0.0) * tangent, axis=1, keepdims=True)
    low_grad = (inv_col * (w_pu - tan_col * q_up)).astype(BF16)
    ga = tn(low_grad, hidden_ref[...])
    pulled = (mixed_ref[...] * (inv_col * inv_col * tan_col)).astype(BF16)
    gb = -tn(low_half, pulled)

    take(wrec, w_sem)
    w = wrec[...]
    loss_ref[...] = jnp.broadcast_to(jnp.sum(jnp.where(lane == LOSS_LANE, w, 0.0)) / (DEVS * Q), (8, 128))
    w_t = jnp.transpose(w)
    for s in range(SLOTS):
        for piece in split(w_t[VOFF + s * RANK : VOFF + (s + 1) * RANK, :], 2):
            gb = gb + nn(piece, picked[s]) * (1.0 / shrink)
    for j in range(WIDTH // 128):
        piece_out[0, pl.ds(j * RANK, RANK), :] = ga[:, j * 128 : (j + 1) * 128]
        piece_out[1, pl.ds(j * RANK, RANK), :] = gb[:, j * 128 : (j + 1) * 128]

    def strew(i, c):
        t = lax.rem(me + 1 + i, DEVS)
        push(piece_out.at[:, pl.ds(t, 1), :], piece_in.at[:, pl.ds(me, 1), :], small_sem.at[9], rs_sem, (t, mp))
        return c

    lax.fori_loop(0, DEVS - 1, strew, 0)
    pltpu.make_async_copy(piece_out.at[:, pl.ds(me, 1), :], piece_in.at[:, pl.ds(me, 1), :], rs_sem).start()

    hi, lo = split(w, 2)
    wide = (iota((DEVS, GROUP), 1) // Q) == lax.rem(iota((DEVS, GROUP), 0), 16)
    for s in range(SLOTS):
        diag[0, s] = jnp.where(wide, nt(hi, folds[s]), 0.0).astype(BF16)
        diag[1, s] = jnp.where(wide, nt(lo, folds[s]), 0.0).astype(BF16)

    def candidates(g_, c):
        rows = pl.ds(pl.multiple_of(g_ * 16, 16), 16)
        d = jnp.concatenate([diag[h, s, rows, :] for h in (0, 1) for s in range(SLOTS)], axis=0)
        o = nn(d, hbuf[pl.ds(pl.multiple_of(g_ * GROUP, 16), GROUP), :])
        o = o[0:48, :] + o[48:96, :]
        for s in range(SLOTS):
            cand[s, rows, :] = o[s * 16 : (s + 1) * 16, :]
        return c

    lax.fori_loop(0, NY, candidates, 0)
    table = jnp.zeros((ROWS, WIDTH), F32)
    for s in range(SLOTS):
        up_at = jnp.concatenate(
            [jnp.zeros((VOFF + s * RANK, WIDTH), F32), up32, jnp.zeros((128 - VOFF - (s + 1) * RANK, WIDTH), F32)], axis=0
        ).astype(BF16)
        cg = (cand[s] + nn(hi, up_at) + nn(lo, up_at)).astype(BF16)
        table = table + tn(pick[s], cg)
    table_ref[...] = table.astype(BF16)

    take(piece_in, rs_sem)
    piece_sum[...] = jnp.sum(piece_in[...], axis=1, keepdims=True)
    final[:, pl.ds(me, 1), :] = piece_sum[...]

    def share(i, c):
        t = lax.rem(me + 1 + i, DEVS)
        push(piece_sum, final.at[:, pl.ds(me, 1), :], small_sem.at[10], ag_sem, (t, mp))
        return c

    lax.fori_loop(0, DEVS - 1, share, 0)
    take(final.at[:, pl.ds(0, DEVS - 1), :], ag_sem)
    for j in range(WIDTH // 128):
        ga_ref[:, pl.ds(j * 128, 128)] = final[0, pl.ds(j * RANK, RANK), :]
        gb_ref[:, pl.ds(j * 128, 128)] = final[1, pl.ds(j * RANK, RANK), :]

    take(hbuf.at[pl.ds(0, (NY * NZ - 1) * CHIP), :], send_sem)
    take(mine, small_sem.at[0])
    take(xb1.at[pl.ds(0, NX - 1)], small_sem.at[1])
    take(lists.at[:, pl.ds(0, 1), :], small_sem.at[2])
    take(xb2.at[pl.ds(0, NX - 1)], small_sem.at[3])
    take(lists.at[:, pl.ds(0, 2 * 7), :], small_sem.at[4])
    take(lists.at[:, pl.ds(0, 2 * NZ * 7), :], small_sem.at[5])
    take(rsx.at[pl.ds(0, NX - 1)], small_sem.at[6])
    home = (me // quarter) == mp

    @pl.when(home)
    def _():
        take(got.at[pl.ds(0, DEVS - 1), :], small_sem.at[7])

    @pl.when(jnp.logical_not(home))
    def _():
        take(got, small_sem.at[7])

    take(wrec.at[pl.ds(0, DEVS - 1), :], small_sem.at[8])
    take(piece_in.at[:, pl.ds(0, DEVS - 1), :], small_sem.at[9])
    take(final.at[:, pl.ds(0, DEVS - 1), :], small_sem.at[10])


def shards(hidden, down, up, passages, ids, storage):
    vm = pl.BlockSpec(memory_space=pltpu.VMEM)
    dma = pltpu.SemaphoreType.DMA
    loss, ga, gb, table = pl.pallas_call(
        kernel,
        out_shape=(
            jax.ShapeDtypeStruct((8, 128), F32),
            jax.ShapeDtypeStruct((RANK, WIDTH), F32),
            jax.ShapeDtypeStruct((RANK, WIDTH), F32),
            jax.ShapeDtypeStruct((ROWS, WIDTH), BF16),
        ),
        in_specs=[pl.BlockSpec(memory_space=pltpu.SMEM), vm, vm, vm, vm, vm],
        out_specs=(vm, vm, vm, vm),
        scratch_shapes=[
            pltpu.VMEM((DEVS * Q, WIDTH), BF16),
            pltpu.VMEM((32, WIDTH), BF16),
            pltpu.VMEM((32, WIDTH), BF16),
            pltpu.VMEM((NX, 40, 128), F32),
            pltpu.VMEM((NX, Q, 128), F32),
            pltpu.VMEM((Q * LISTED, 128), F32),
            pltpu.VMEM((2, DEVS, 128), F32),
            pltpu.VMEM((SLOTS, DEVS, ROWS), BF16),
            pltpu.VMEM((SLOTS, DEVS, WIDTH), BF16),
            pltpu.VMEM((SLOTS, GROUP, 128), BF16),
            pltpu.VMEM((2, SLOTS, DEVS, GROUP), BF16),
            pltpu.VMEM((NX, DEVS // NX, 128), F32),
            pltpu.VMEM((DEVS, 128), F32),
            pltpu.VMEM((DEVS // NX, 128), F32),
            pltpu.VMEM((DEVS, 128), F32),
            pltpu.VMEM((DEVS, 128), F32),
            pltpu.VMEM((DEVS, 128), F32),
            pltpu.VMEM((SLOTS, DEVS, WIDTH), F32),
            pltpu.VMEM((2, DEVS, 128), F32),
            pltpu.VMEM((2, DEVS, 128), F32),
            pltpu.VMEM((2, 1, 128), F32),
            pltpu.VMEM((2, DEVS, 128), F32),
            pltpu.VMEM((Q, WIDTH), F32),
            dma, dma, dma, dma,
            dma((NZ,)), dma((NY,)),
            dma((NY * NZ,)), dma((NY * NZ,)),
            dma, dma, dma, dma, dma,
            dma, dma((11,)),
        ],
        compiler_params=pltpu.CompilerParams(collective_id=0, has_side_effects=True, vmem_limit_bytes=56 << 20),
        name="contrastive",
    )(ids, hidden, down, up, passages, storage.reshape(ROWS, 128))
    return loss[0, 0], ga, gb, table


def solution(mesh):
    return jax.shard_map(
        shards,
        mesh=mesh,
        in_specs=(P("dp", "mp"), P(None, "mp"), P(None, "mp"), P("dp", "mp"), P("dp", None), P()),
        out_specs=(P(), P(None, "mp"), P(None, "mp"), P("dp", "mp")),
        check_vma=False,
    )
```

time: 422 us -> 106 us (0.25)
  blocking collectives: 325 us -> 0 us
  Pallas kernels: 0 us -> 98.8 us
  local copies, waits for them, and re-layouts: 40.3 us -> 6.75 us
  starting transfers between devices: 16.6 us -> 0 us
  between operations: 16.1 us -> 0.64 us
  waiting for transfers between devices: 12.5 us -> 0 us
  other arithmetic: 8.81 us -> 0 us
    psum x6 -> x0, blocking collectives: 295 us -> none  [the longest x1 251 us: shards(): lax.psum((grad_a_part, grad_b_part, jnp.sum(loss_rows)), 'dp')]
    pallas_call x0 -> x1, Pallas kernels: none -> 98.8 us  [shards(): pl.pallas_call(kernel, out_shape=(jax.ShapeDtypeStruct((8, 128), F32), ja...]
    all_to_all x1 -> x0, blocking collectives: 29.7 us -> none  [shards(): lax.all_to_all(wanted, 'dp', split_axis=0, concat_axis=0, tiled=True)]
    scatter x3 -> x0, local copies, waits for them, and re-layouts: 23.7 us -> none  [the longest x2 14.4 us: shards(): outgoing = jnp.zeros((data_count, capacity, feature_columns), jnp.bfloat1...]
    all_to_all x2 -> x0, starting transfers between devices: 16.6 us -> none  [the longest x1 10.8 us: shards(): lax.all_to_all(outgoing, 'dp', split_axis=0, concat_axis=0, tiled=True)]
    all_to_all x2 -> x0, waiting for transfers between devices: 12.5 us -> none  [the longest x1 12.5 us: send_rows(): lax.all_to_all(found_rows, 'dp', split_axis=0, concat_axis=0, tiled=True)]
    gather x4 -> x0, local copies, waits for them, and re-layouts: 7.96 us -> none  [the longest x1 3.21 us: shards(): candidates = returned[owners, slot_index]]
    scatter-add x1 -> x0, other arithmetic: 4.88 us -> none  [shards(): table_grad = jnp.zeros((resident, feature_columns), jnp.float32).at[serve...]
  transfers between devices with their start and end apart: 3 -> 0, of which waited for: 1 -> 0; matrix products, arithmetic and copies ran while one was open for 3% -> 0% of each run, Pallas kernels for 0% -> 0%
where the time goes in v1:
time: 106 us
  Pallas kernels  98.8 us (93%)
  local copies, waits for them, and re-layouts  6.75 us (6%)
    pallas_call x1, Pallas kernels, shards(): pl.pallas_call(kernel, out_shape=(jax.ShapeDtypeStruct((8, 128), F32), ja...  98.8 us
    unnamed x6, local copies, waits for them, and re-layouts  5.56 us

profile of v1, /device:TPU:1, one launch (start us, length us, event | category | flops | bytes accessed | tf_op | source)
XLA Modules:
  0.0 106.1 jit_solution(5565186091766373945)
XLA Ops:
  0.6 1.4 %copy.10.ids_ref = s32[24,8]{1,0:T(8,128)} copy(s32[24,8]{0,1:T(8,128)} %param.10) | data formatting | bytes 1536 | tf_op args[4]
  2.0 98.8 %contrastive.1 = (f32[8,128]{1,0:T(8,128)}, f32[16,1024]{1,0:T(8,128)}, f32[16,1024]{1,0:T(8,128)}, bf16[384,1024]{1,0:T(8,128)(2,1)}) custom-call(s32[24,8]{1,0:T(8,128)} %copy.10.ids_ref, bf16[24,1024]{1,0:T(8,128)(2,1)} %hidden_ref.1, bf16[16,1024]{1,0:T(8,128)(2,1)} %down_ref.1, bf16[16,1024]{1,0:T(8,128)(2,1)} %up_ref.1, bf16[384,1024]{1,0:T(8,128)(2,1)} %pass_ref.1, ...), custom_call_target="tpu_custom_call" | custom-call | tf_op jit(solution)/shard_map/contrastive/pallas_call | solution.py:461
  100.8 1.2 %slice.3 = f32[1,1]{1,0:T(1,128)} slice(f32[8,128]{1,0:T(8,128)} %get-tuple-element.8), slice={[0:1], [0:1]} | slice | bytes 8 | tf_op jit(solution)/shard_map/slice | solution.py:504
  101.9 0.0 copy-start
  101.9 1.5 %copy.14 = f32[16,1024]{1,0:T(8,128)} copy(f32[16,1024]{1,0:T(8,128)} %get-tuple-element.17) | data formatting | bytes 131072
  103.4 0.0 copy-done
  103.4 0.6 copy.15
  104.1 2.1 %copy.16 = bf16[384,1024]{1,0:T(8,128)(2,1)} copy(bf16[384,1024]{1,0:T(8,128)(2,1)} %get-tuple-element.19) | data formatting | bytes 1572864
Async XLA Ops:
  101.9 1.5 %copy-start = (f32[16,1024]{1,0:T(8,128)S(1)}, f32[16,1024]{1,0:T(8,128)}, u32[]{:S(2)}) copy-start(f32[16,1024]{1,0:T(8,128)} %get-tuple-element.18) | copy-start | bytes 196612

commit v2 on v1

--- a/solution.py
+++ b/solution.py
@@ -60,12 +60,12 @@
 
 
 def kernel(
-    ids_ref, hidden_ref, down_ref, up_ref, pass_ref, storage_ref,
-    loss_ref, ga_ref, gb_ref, table_ref,
+    ids_ref, hidden_ref, down_ref, up_ref, pass_hbm, storage_hbm,
+    loss_ref, pieces_ref, table_hbm,
     hbuf, mine, theirs, xb1, xb2, locs, lists, pick, picked, folds, diag, rsx, part, summed, got, back, wrec,
-    cand, piece_out, piece_in, piece_sum, final, mixed_ref,
-    st_sem, e1_sem, e2_sem, l_sem, lz_sem, ly_sem, ring_sem, sib_sem, rsx_sem, got_sem, w_sem, rs_sem, ag_sem,
-    send_sem, small_sem,
+    cand, piece_out, piece_in, piece_sum, final, mixed_ref, pass_ref, storage_ref, table_ref,
+    st_sem, e1_sem, e2_sem, l_sem, lz_sem, ly_sem, line_sem, ring_sem, sib_sem, rsx_sem, got_sem, w_sem, rs_sem, ag_sem,
+    send_sem, small_sem, load_sem,
 ):
     me, mp = lax.axis_index("dp"), lax.axis_index("mp")
     core, chip_me = lax.rem(me, 2), me // 2
@@ -84,30 +84,107 @@
 
     sibling = (chip_me * 2 + 1 - core, mp)
 
+    sa, sb = NZ - (NZ - 1) * core, 1 + (NZ - 1) * core
+    a = jnp.where(core == 0, y, z)
+    b = jnp.where(core == 0, z, y)
+
+    def line_dev(o):
+        return (lax.rem(a + o + NY, NY) * sa + b * sb) * 2 + core
+
+    def cross_dev(o):
+        return (a * sa + lax.rem(b + o + NY, NY) * sb) * 2 + core
+
+    loads = [
+        pltpu.make_async_copy(storage_hbm, storage_ref, load_sem.at[0]),
+        pltpu.make_async_copy(pass_hbm, pass_ref, load_sem.at[1]),
+    ]
+    for cp in loads:
+        cp.start()
+
     bar = pltpu.get_barrier_semaphore()
-    for t in (dev(y + 1, z, core), dev(y - 1, z, core), dev(y, z + 1, core), dev(y, z - 1, core), sibling):
-        pl.semaphore_signal(bar, inc=1, device_id=t, device_id_type=MESH)
+    for o in (4, 3, 5, 2, 6, 1, 7):
+        pl.semaphore_signal(bar, inc=1, device_id=(line_dev(o), mp), device_id_type=MESH)
+        pl.semaphore_signal(bar, inc=1, device_id=(cross_dev(o), mp), device_id_type=MESH)
+    pl.semaphore_signal(bar, inc=1, device_id=sibling, device_id_type=MESH)
     for i in range(1, NX):
         pl.semaphore_signal(bar, inc=1, device_id=(me, lax.rem(mp + i, NX)), device_id_type=MESH)
 
     hid32 = hidden_ref[...].astype(F32)
+    mine[...] = jnp.concatenate([hid32, jnp.zeros((8, WIDTH), F32)], axis=0).astype(BF16)
+    pl.semaphore_wait(bar, NY - 1 + NZ - 1 + 1 + NX - 1)
+    push(mine, theirs, small_sem.at[0], st_sem, sibling)
+
     up32 = up_ref[...].astype(F32)
-    mine[...] = jnp.concatenate([hid32, jnp.zeros((8, WIDTH), F32)], axis=0).astype(BF16)
     left = jnp.concatenate([hid32, up32], axis=0).astype(BF16)
     right = jnp.concatenate([down_ref[...].astype(F32), up32, jnp.zeros((96, WIDTH), F32)], axis=0).astype(BF16)
     prod = nt(left, right)
+
+    take(theirs, st_sem)
+    theirs32 = theirs[0:Q, :].astype(F32)
+    both = jnp.where(core == 0, jnp.concatenate([hid32, theirs32], axis=0), jnp.concatenate([theirs32, hid32], axis=0))
+    hbuf[y, z] = both.astype(BF16)
+
+    far = sorted((o for o in range(-3, 5) if o), key=abs, reverse=True)
+
+    def bundle(c, p, bb):
+        lanes = pl.ds(c * HALF, HALF)
+        if c == 0:
+            return hbuf.at[pl.ds(2 * p, 2), bb, :, lanes]
+        return hbuf.at[bb, pl.ds(2 * p, 2), :, lanes]
+
+    def single(c, aa, bb):
+        lanes = pl.ds(c * HALF, HALF)
+        return hbuf.at[aa, bb, :, lanes] if c == 0 else hbuf.at[bb, aa, :, lanes]
+
+    pair = a // 2
+    pairs = [lax.rem(pair + o, 4) for o in (0, 1, 3, 2)]
+
+    def line_start(c):
+        r = single(c, a, b)
+        for o in far:
+            push(r, r, send_sem, line_sem.at[pair], (line_dev(o), mp))
+
+    def line_done(c, k):
+        p = pairs[k]
+        if k == 0:
+            r = single(c, 2 * pair + 1 - lax.rem(a, 2), b)
+        else:
+            r = bundle(c, p, b)
+        take(r, line_sem.at[p])
+        both_chips = bundle(c, p, b)
+        for o in (1, -1):
+            push(both_chips, both_chips, send_sem, ring_sem.at[p, b], (cross_dev(o), mp))
+        push(r, r, send_sem, sib_sem.at[p, b], sibling)
+
+    def ring_event(c, k, t):
+        p = pairs[k]
+        for d in (1, -1):
+            last = 4 if (k % 2 == 0) == (d > 0) else 3
+            if t > last:
+                continue
+            bb = lax.rem(b - d * t + 2 * NY, NY)
+            r = bundle(c, p, bb)
+            take(r, ring_sem.at[p, bb])
+            if t < last:
+                push(r, r, send_sem, ring_sem.at[p, bb], (cross_dev(d), mp))
+            push(r, r, send_sem, sib_sem.at[p, bb], sibling)
+
+    for c in (0, 1):
+        @pl.when(core == c)
+        def _():
+            line_start(c)
+
+    loads[1].wait()
     biggest = jnp.max(jnp.max(jnp.abs(pass_ref[...].astype(F32)), axis=0, keepdims=True), axis=1, keepdims=True)
     lane40, row40 = iota((40, 128), 1), iota((40, 128), 0)
     xb1[mp] = jnp.where((lane40 == 40) & (row40 == 0), biggest, prod)
-
-    pl.semaphore_wait(bar, 5 + NX - 1)
-    push(mine, theirs, small_sem.at[0], st_sem, sibling)
     for i in range(1, NX):
         push(xb1.at[mp], xb1.at[mp], small_sem.at[1], e1_sem, (me, lax.rem(mp + i, NX)))
 
+    loads[0].wait()
     lane1 = iota((1, 128), 1)
     for j in range(Q * LISTED):
-        pid = ids_ref[j // LISTED, j % LISTED]
+        pid = ids_ref[j % LISTED, j // LISTED]
         row = storage_ref[pl.ds(pid // 128, 1), :]
         locs[pl.ds(j, 1), :] = jnp.where(lane1 == lax.rem(pid, 128), row, 0).astype(F32)
     located = jnp.sum(locs[...], axis=1, keepdims=True)
@@ -118,56 +195,43 @@
     lists[1, pl.ds(me, 1), :] = as_row[:, 128:256]
     push(lists.at[:, pl.ds(me, 1), :], lists.at[:, pl.ds(me, 1), :], small_sem.at[2], l_sem, sibling)
 
-    take(theirs, st_sem)
-    theirs32 = theirs[0:Q, :].astype(F32)
-    both = jnp.where(core == 0, jnp.concatenate([hid32, theirs32], axis=0), jnp.concatenate([theirs32, hid32], axis=0))
-    hbuf[pl.ds(pl.multiple_of(chip_me * CHIP, 16), CHIP), :] = both.astype(BF16)
-
-    sa, sb = NZ - (NZ - 1) * core, 1 + (NZ - 1) * core
-    a = jnp.where(core == 0, y, z)
-    b = jnp.where(core == 0, z, y)
-    lanes = pl.ds(pl.multiple_of(core * HALF, HALF), HALF)
-
-    def chip_of(aa, bb):
-        return lax.rem(aa + 2 * NY, NY) * sa + lax.rem(bb + 2 * NY, NY) * sb
-
-    def region(ci):
-        return hbuf.at[pl.ds(pl.multiple_of(ci * CHIP, 16), CHIP), lanes]
-
-    def pass_on(ci, target, rsem):
-        push(region(ci), region(ci), send_sem, rsem, target)
-
-    ar, al = (chip_of(a + 1, b) * 2 + core, mp), (chip_of(a - 1, b) * 2 + core, mp)
-    br, bl = (chip_of(a, b + 1) * 2 + core, mp), (chip_of(a, b - 1) * 2 + core, mp)
-    order = [0, -1, 1, -2, 2, -3, 3, -4]
-
-    def steps(j, d):
-        return 4 if (j % 2 == 0) == (d > 0) else 3
-
-    def event(j, t):
-        off = order[j]
-        if t == 0:
-            ci = chip_of(a + off, b)
-            if j > 0:
-                take(region(ci), ring_sem.at[ci])
-            if j == 0 or (off < 0 and off > -4):
-                pass_on(ci, ar, ring_sem.at[ci])
-            if j == 0 or (off > 0 and off < 3):
-                pass_on(ci, al, ring_sem.at[ci])
-            pass_on(ci, br, ring_sem.at[ci])
-            pass_on(ci, bl, ring_sem.at[ci])
-            if j > 0:
-                pass_on(ci, sibling, sib_sem.at[ci])
-        else:
-            for d in (1, -1):
-                if t <= steps(j, d):
-                    ci = chip_of(a + off, b - d * t)
-                    take(region(ci), ring_sem.at[ci])
-                    if t < steps(j, d):
-                        pass_on(ci, br if d > 0 else bl, ring_sem.at[ci])
-                    pass_on(ci, sibling, sib_sem.at[ci])
-
-    event(0, 0)
+    take(lists.at[:, pl.ds(0, 1), :], l_sem)
+
+    def some_lists(first, n):
+        return lists.at[:, pl.ds(pl.multiple_of(first, 2), n), :]
+
+    for o in (4, 3, 5, 2, 6, 1, 7):
+        r = some_lists(chip_me * 2, 2)
+        push(r, r, small_sem.at[4], lz_sem.at[z], dev(y, z + o, core))
+
+    def lists_on():
+        def each(i, c):
+            zz = lax.rem(z + i, NZ)
+            take(some_lists((y * NZ + zz) * 2, 2), lz_sem.at[zz])
+            return c
+        lax.fori_loop(1, NZ, each, 0)
+        for o in (4, 3, 5, 2, 6, 1, 7):
+            r = some_lists(y * 2 * NZ, 2 * NZ)
+            push(r, r, small_sem.at[5], ly_sem.at[y], dev(y + o, z, core))
+
+    def lists_done():
+        def each(i, c):
+            yy = lax.rem(y + i, NY)
+            take(some_lists(yy * 2 * NZ, 2 * NZ), ly_sem.at[yy])
+            return c
+        lax.fori_loop(1, NY, each, 0)
+
+    def ring(first, last):
+        for c in (0, 1):
+            @pl.when(core == c)
+            def _():
+                for n in range(first, last):
+                    if n < 4:
+                        line_done(c, n)
+                    else:
+                        ring_event(c, n % 4, n // 4)
+
+    ring(0, 6)
 
     take(xb1.at[pl.ds(0, NX - 1)], e1_sem)
     tot = xb1[0] + xb1[1] + xb1[2] + xb1[3]
@@ -183,56 +247,20 @@
     for i in range(1, NX):
         push(xb2.at[mp], xb2.at[mp], small_sem.at[3], e2_sem, (me, lax.rem(mp + i, NX)))
 
-    take(lists.at[:, pl.ds(0, 1), :], l_sem)
-
-    def line(ref_rows, n):
-        return lists.at[:, pl.ds(ref_rows, n), :]
-
-    zr, zl = dev(y, z + 1, core), dev(y, z - 1, core)
-    yr, yl = dev(y + 1, z, core), dev(y - 1, z, core)
-
-    def list_step(t):
-        if t <= 4:
-            for d, to in ((1, zr), (-1, zl)):
-                lim = 4 if d > 0 else 3
-                if t > lim:
-                    continue
-                zz = lax.rem(z - d * t + 2 * NZ, NZ)
-                rows = pl.multiple_of((y * NZ + zz) * 2, 2)
-                if t > 0:
-                    take(line(rows, 2), lz_sem.at[zz])
-                if t < lim:
-                    push(line(rows, 2), line(rows, 2), small_sem.at[4], lz_sem.at[zz], to)
-        if t >= 4:
-            u = t - 4
-            for d, to in ((1, yr), (-1, yl)):
-                lim = 4 if d > 0 else 3
-                if u > lim:
-                    continue
-                yy = lax.rem(y - d * u + 2 * NY, NY)
-                rows = pl.multiple_of(yy * 2 * NZ, 2 * NZ)
-                if u > 0:
-                    take(line(rows, 2 * NZ), ly_sem.at[yy])
-                if u < lim:
-                    push(line(rows, 2 * NZ), line(rows, 2 * NZ), small_sem.at[5], ly_sem.at[yy], to)
-
-    list_step(0)
-
-    events = sorted((j + 2 * t, t, j) for j in range(8) for t in range(5) if j + t > 0)
-    sections = {}
-    for n, (key, t, j) in enumerate(events):
-        event(j, t)
-        if n % 4 == 3 and n // 4 + 1 <= 8:
-            list_step(n // 4 + 1)
+    ring(6, 8)
+    lists_on()
+    ring(8, 14)
 
     take(xb2.at[pl.ds(0, NX - 1)], e2_sem)
     inv_norm = lax.rsqrt((xb2[0] + xb2[1] + xb2[2] + xb2[3]) / (WIDTH * NX) + EPSILON)
+
+    ring(14, 16)
+    lists_done()
 
     wanted = jnp.concatenate([lists[0], lists[1]], axis=1) - (me * ROWS).astype(F32)
     here = (wanted >= 0.0) & (wanted < ROWS)
     earlier = nn(here.astype(F32).astype(BF16), (r256 < l256).astype(F32).astype(BF16))
     rows_iota = iota((DEVS, ROWS), 1).astype(F32)
-    group_mask = (iota((SLOTS * 16, GROUP), 1) // Q) == lax.rem(iota((SLOTS * 16, GROUP), 0), 16)
     part_pu = jnp.zeros((DEVS, 128), F32)
     for s in range(SLOTS):
         col = jnp.sum(jnp.where(here & (earlier == s), wanted + 1.0, 0.0), axis=1, keepdims=True) - 1.0
@@ -267,28 +295,44 @@
     spread = jnp.where(same_slot, spread, 0.0).astype(BF16)
     inv_lane = jnp.sum(inv_norm * at_query, axis=0, keepdims=True)
 
-    def rest(i, c):
-        @pl.when(i != chip_me)
+    ring(16, 20)
+
+    def rest(c):
+        for p in range(4):
+            def each(bb, carry, p=p):
+                both_chips = bundle(c, p, bb)
+                at_home = bb == a
+
+                @pl.when(at_home & (b // 2 == p))
+                def _():
+                    take(single(c, 2 * p, bb), sib_sem.at[p, bb])
+
+                @pl.when(jnp.logical_not(at_home & (b // 2 == p)))
+                def _():
+                    take(both_chips, sib_sem.at[p, bb])
+                return carry
+            lax.fori_loop(0, NY, each, 0)
+
+    for c in (0, 1):
+        @pl.when(core == c)
         def _():
-            r = hbuf.at[pl.ds(pl.multiple_of(i * CHIP, 16), CHIP), pl.ds(pl.multiple_of(HALF - core * HALF, HALF), HALF)]
-            take(r, sib_sem.at[i])
-        return c
-
-    lax.fori_loop(0, NY * NZ, rest, 0)
+            rest(1 - c)
+
+    lane48 = lax.rem(iota((Q, SLOTS * 16), 1), 16)
 
     def score(g, c):
         rows = pl.ds(pl.multiple_of(g * 16, 16), 16)
         s_g = jnp.concatenate([picked[s, rows, :] for s in range(SLOTS)], axis=0)
-        d = nt(s_g, hbuf[pl.ds(pl.multiple_of(g * GROUP, 16), GROUP), :])
-        d = jnp.where(group_mask, d, 0.0)
-        acc = jnp.zeros((16, 128), F32)
-        for s in range(SLOTS):
-            for piece in split(d[s * 16 : (s + 1) * 16, :], 3):
-                acc = acc + nn(piece, folds[s])
-        part[rows, :] = acc
+        d = nt(hbuf[g].reshape(GROUP, WIDTH), s_g)
+        e = jnp.zeros((Q, SLOTS * 16), F32)
+        for r in range(16):
+            e = e + jnp.where(lane48 == r, d[r * Q : (r + 1) * Q, :], 0.0)
+        e = jnp.concatenate([e, jnp.zeros((Q, 128 - SLOTS * 16), F32)], axis=1)
+        e = jnp.transpose(jnp.concatenate([e, jnp.zeros((128 - Q, 128), F32)], axis=0))
+        part[rows, :] = e[0:16, :] + pltpu.roll(e[16:32, :], Q, 1) + pltpu.roll(e[32:48, :], 2 * Q, 1)
         return c
 
-    lax.fori_loop(0, NY, score, 0)
+    lax.fori_loop(0, NY, score, 0, unroll=True)
     part[...] = part[...] + part_pu + jnp.where(lane == G_LANE, shrink * (1.0 / NX), 0.0)
 
     quarter = DEVS // NX
@@ -303,25 +347,48 @@
     take(rsx.at[pl.ds(0, NX - 1)], rsx_sem)
     summed[...] = rsx[0] + rsx[1] + rsx[2] + rsx[3]
 
-    def give(i, c):
-        j = lax.rem(i + me, quarter)
-        block = mp * quarter + j
-        for dk in range(NX):
-            k = lax.rem(mp + dk, NX)
+    def swing(m):
+        return ((8 - m) // 2) * (2 * lax.rem(m, 2) - 1)
+
+    def far_first(m):
+        return ((8 - m) // 2) * (1 if m % 2 else -1)
+
+    def to_all(send):
+        inner = [lax.rem(z + far_first(n) + NZ, NZ) * 2 + c for n in range(NZ) for c in (1 - core, core)]
+
+        def far_rows(m, carry):
+            base = lax.rem(y + swing(m) + NY, NY) * (2 * NZ)
+            for n in inner:
+                send(base + n)
+            return carry
+
+        lax.fori_loop(0, NY - 1, far_rows, 0)
+        for n in inner[:-1]:
+            send(y * (2 * NZ) + n)
+
+    home = (me // quarter) == mp
+
+    others = [lax.rem(mp + dk, NX) for dk in (2, 1, 3)]
+
+    def give(m, c):
+        first = lax.rem(z + swing(m) + NZ, NZ) * 2
+        for j in (first, first + 1, first + 2 * NZ, first + 2 * NZ + 1):
+            block = mp * quarter + j
             src = summed.at[pl.ds(j, 1), :]
-            if dk == 0:
-                @pl.when(block == me)
-                def _():
-                    pltpu.make_async_copy(src, got.at[pl.ds(me, 1), :], got_sem).start()
-
-                @pl.when(block != me)
-                def _():
-                    push(src, got.at[pl.ds(me, 1), :], small_sem.at[7], got_sem, (block, k))
-            else:
+            for k in others:
                 push(src, got.at[pl.ds(me, 1), :], small_sem.at[7], got_sem, (block, k))
+
+            @pl.when(block != me)
+            def _():
+                push(src, got.at[pl.ds(me, 1), :], small_sem.at[7], got_sem, (block, mp))
         return c
 
-    lax.fori_loop(0, quarter, give, 0)
+    lax.fori_loop(0, NZ, give, 0)
+
+    @pl.when(home)
+    def _():
+        pltpu.make_async_copy(summed.at[pl.ds(lax.rem(me, quarter), 1), :], got.at[pl.ds(me, 1), :], got_sem).start()
+
     take(got, got_sem)
 
     g = got[...]
@@ -352,12 +419,7 @@
         v = v + nt(piece, spread)
     back[...] = w2 + v + jnp.where(lane == LOSS_LANE, loss, 0.0)
 
-    def hand(i, c):
-        t = lax.rem(me + 1 + i, DEVS)
-        push(back.at[pl.ds(t, 1), :], wrec.at[pl.ds(me, 1), :], small_sem.at[8], w_sem, (t, mp))
-        return c
-
-    lax.fori_loop(0, DEVS - 1, hand, 0)
+    to_all(lambda t: push(back.at[pl.ds(t, 1), :], wrec.at[pl.ds(me, 1), :], small_sem.at[8], w_sem, (t, mp)))
     pltpu.make_async_copy(back.at[pl.ds(me, 1), :], wrec.at[pl.ds(me, 1), :], w_sem).start()
 
     z_all = exact(((0,), (0,)), weights, ranks * unshrink)
@@ -375,7 +437,7 @@
 
     take(wrec, w_sem)
     w = wrec[...]
-    loss_ref[...] = jnp.broadcast_to(jnp.sum(jnp.where(lane == LOSS_LANE, w, 0.0)) / (DEVS * Q), (8, 128))
+    loss_ref[...] = jnp.sum(jnp.sum(jnp.where(lane == LOSS_LANE, w, 0.0), axis=0, keepdims=True), axis=1, keepdims=True) / (DEVS * Q)
     w_t = jnp.transpose(w)
     for s in range(SLOTS):
         for piece in split(w_t[VOFF + s * RANK : VOFF + (s + 1) * RANK, :], 2):
@@ -384,12 +446,7 @@
         piece_out[0, pl.ds(j * RANK, RANK), :] = ga[:, j * 128 : (j + 1) * 128]
         piece_out[1, pl.ds(j * RANK, RANK), :] = gb[:, j * 128 : (j + 1) * 128]
 
-    def strew(i, c):
-        t = lax.rem(me + 1 + i, DEVS)
-        push(piece_out.at[:, pl.ds(t, 1), :], piece_in.at[:, pl.ds(me, 1), :], small_sem.at[9], rs_sem, (t, mp))
-        return c
-
-    lax.fori_loop(0, DEVS - 1, strew, 0)
+    to_all(lambda t: push(piece_out.at[:, pl.ds(t, 1), :], piece_in.at[:, pl.ds(me, 1), :], small_sem.at[9], rs_sem, (t, mp)))
     pltpu.make_async_copy(piece_out.at[:, pl.ds(me, 1), :], piece_in.at[:, pl.ds(me, 1), :], rs_sem).start()
 
     hi, lo = split(w, 2)
@@ -401,7 +458,7 @@
     def candidates(g_, c):
         rows = pl.ds(pl.multiple_of(g_ * 16, 16), 16)
         d = jnp.concatenate([diag[h, s, rows, :] for h in (0, 1) for s in range(SLOTS)], axis=0)
-        o = nn(d, hbuf[pl.ds(pl.multiple_of(g_ * GROUP, 16), GROUP), :])
+        o = nn(d, hbuf[g_].reshape(GROUP, WIDTH))
         o = o[0:48, :] + o[48:96, :]
         for s in range(SLOTS):
             cand[s, rows, :] = o[s * 16 : (s + 1) * 16, :]
@@ -416,23 +473,23 @@
         cg = (cand[s] + nn(hi, up_at) + nn(lo, up_at)).astype(BF16)
         table = table + tn(pick[s], cg)
     table_ref[...] = table.astype(BF16)
+    table_out = pltpu.make_async_copy(table_ref, table_hbm, load_sem.at[2])
+    table_out.start()
 
     take(piece_in, rs_sem)
     piece_sum[...] = jnp.sum(piece_in[...], axis=1, keepdims=True)
     final[:, pl.ds(me, 1), :] = piece_sum[...]
 
-    def share(i, c):
-        t = lax.rem(me + 1 + i, DEVS)
-        push(piece_sum, final.at[:, pl.ds(me, 1), :], small_sem.at[10], ag_sem, (t, mp))
-        return c
-
-    lax.fori_loop(0, DEVS - 1, share, 0)
+    to_all(lambda t: push(piece_sum, final.at[:, pl.ds(me, 1), :], small_sem.at[10], ag_sem, (t, mp)))
     take(final.at[:, pl.ds(0, DEVS - 1), :], ag_sem)
-    for j in range(WIDTH // 128):
-        ga_ref[:, pl.ds(j * 128, 128)] = final[0, pl.ds(j * RANK, RANK), :]
-        gb_ref[:, pl.ds(j * 128, 128)] = final[1, pl.ds(j * RANK, RANK), :]
-
-    take(hbuf.at[pl.ds(0, (NY * NZ - 1) * CHIP), :], send_sem)
+    pieces_ref[...] = final[...]
+    table_out.wait()
+
+    half = pl.ds(0, HALF)
+    take(hbuf.at[0, pl.ds(0, 7), :, half], send_sem)
+    take(hbuf.at[pl.ds(0, 7), :, :, half], send_sem)
+    take(hbuf.at[0, pl.ds(0, 7), :, half], send_sem)
+    take(hbuf.at[pl.ds(0, 7), :, :, half], send_sem)
     take(mine, small_sem.at[0])
     take(xb1.at[pl.ds(0, NX - 1)], small_sem.at[1])
     take(lists.at[:, pl.ds(0, 1), :], small_sem.at[2])
@@ -440,8 +497,6 @@
     take(lists.at[:, pl.ds(0, 2 * 7), :], small_sem.at[4])
     take(lists.at[:, pl.ds(0, 2 * NZ * 7), :], small_sem.at[5])
     take(rsx.at[pl.ds(0, NX - 1)], small_sem.at[6])
-    home = (me // quarter) == mp
-
     @pl.when(home)
     def _():
         take(got.at[pl.ds(0, DEVS - 1), :], small_sem.at[7])
@@ -455,21 +510,25 @@
     take(final.at[:, pl.ds(0, DEVS - 1), :], small_sem.at[10])
 
 
+def finish(loss_in, pieces_ref, table_in, loss_ref, ga_ref, gb_ref, table_out):
+    table_out[...] = table_in[...]
+    loss_ref[...] = loss_in[...]
+    for j in range(WIDTH // 128):
+        ga_ref[:, pl.ds(j * 128, 128)] = pieces_ref[0, pl.ds(j * RANK, RANK), :]
+        gb_ref[:, pl.ds(j * 128, 128)] = pieces_ref[1, pl.ds(j * RANK, RANK), :]
+
+
 def shards(hidden, down, up, passages, ids, storage):
-    vm = pl.BlockSpec(memory_space=pltpu.VMEM)
+    vm, hbm = pl.BlockSpec(memory_space=pltpu.VMEM), pl.BlockSpec(memory_space=pl.ANY)
     dma = pltpu.SemaphoreType.DMA
-    loss, ga, gb, table = pl.pallas_call(
+    shape = jax.ShapeDtypeStruct
+    loss, pieces, table = pl.pallas_call(
         kernel,
-        out_shape=(
-            jax.ShapeDtypeStruct((8, 128), F32),
-            jax.ShapeDtypeStruct((RANK, WIDTH), F32),
-            jax.ShapeDtypeStruct((RANK, WIDTH), F32),
-            jax.ShapeDtypeStruct((ROWS, WIDTH), BF16),
-        ),
-        in_specs=[pl.BlockSpec(memory_space=pltpu.SMEM), vm, vm, vm, vm, vm],
-        out_specs=(vm, vm, vm, vm),
+        out_shape=(shape((1, 1), F32), shape((2, DEVS, 128), F32), shape((ROWS, WIDTH), BF16)),
+        in_specs=[pl.BlockSpec(memory_space=pltpu.SMEM), vm, vm, vm, hbm, hbm],
+        out_specs=(vm, vm, hbm),
         scratch_shapes=[
-            pltpu.VMEM((DEVS * Q, WIDTH), BF16),
+            pltpu.VMEM((NY, NZ, CHIP, WIDTH), BF16),
             pltpu.VMEM((32, WIDTH), BF16),
             pltpu.VMEM((32, WIDTH), BF16),
             pltpu.VMEM((NX, 40, 128), F32),
@@ -492,16 +551,26 @@
             pltpu.VMEM((2, 1, 128), F32),
             pltpu.VMEM((2, DEVS, 128), F32),
             pltpu.VMEM((Q, WIDTH), F32),
+            pltpu.VMEM((ROWS, WIDTH), BF16),
+            pltpu.VMEM((ROWS, 128), jnp.int32),
+            pltpu.VMEM((ROWS, WIDTH), BF16),
             dma, dma, dma, dma,
             dma((NZ,)), dma((NY,)),
-            dma((NY * NZ,)), dma((NY * NZ,)),
+            dma((4,)), dma((4, NY)), dma((4, NY)),
             dma, dma, dma, dma, dma,
-            dma, dma((11,)),
+            dma, dma((11,)), dma((3,)),
         ],
         compiler_params=pltpu.CompilerParams(collective_id=0, has_side_effects=True, vmem_limit_bytes=56 << 20),
         name="contrastive",
-    )(ids, hidden, down, up, passages, storage.reshape(ROWS, 128))
-    return loss[0, 0], ga, gb, table
+    )(ids.T, hidden, down, up, passages, storage.reshape(ROWS, 128))
+    loss, ga, gb, table = pl.pallas_call(
+        finish,
+        out_shape=(shape((1, 1), F32), shape((RANK, WIDTH), F32), shape((RANK, WIDTH), F32), shape((ROWS, WIDTH), BF16)),
+        in_specs=[vm, vm, vm],
+        out_specs=(vm, vm, vm, vm),
+        name="finish",
+    )(loss, pieces, table)
+    return loss.reshape(()), ga, gb, table
 
 
 def solution(mesh):

time: 106 us -> 87.6 us (0.83)
  Pallas kernels: 98.8 us -> 86.8 us
  local copies, waits for them, and re-layouts: 6.75 us -> 0 us
    pallas_call x1 -> x2, Pallas kernels: 98.8 us -> 86.8 us  [the longest x1 84 us: shards(): pl.pallas_call(kernel, out_shape=(shape((1, 1), F32), shape((2, DEVS, 128...]
    unnamed x6 -> x0, local copies, waits for them, and re-layouts: 5.56 us -> none
    slice x1 -> x0, local copies, waits for them, and re-layouts: 1.19 us -> none  [shards(): return (loss[0, 0], ga, gb, table)]
where the time goes in v2:
time: 87.6 us; the launch traced here: 87.4 us
  Pallas kernels  86.8 us (99%)
    pallas_call x1, Pallas kernels, shards(): pl.pallas_call(kernel, out_shape=(shape((1, 1), F32), shape((2, DEVS, 128...  84 us
    pallas_call x1, Pallas kernels, shards(): pl.pallas_call(finish, out_shape=(shape((1, 1), F32), shape((RANK, WIDTH)...  2.78 us

profile of v2, /device:TPU:1, one launch (start us, length us, event | category | flops | bytes accessed | tf_op | source)
XLA Modules:
  0.0 87.4 jit_solution(18031156817024650491)
XLA Ops:
  0.6 84.0 %contrastive.1 = (f32[1,1]{1,0:T(1,128)}, f32[2,128,128]{2,1,0:T(8,128)}, bf16[384,1024]{1,0:T(8,128)(2,1)}) custom-call(s32[8,24]{1,0:T(8,128)} %bitcast.4, bf16[24,1024]{1,0:T(8,128)(2,1)} %hidden_ref.1, bf16[16,1024]{1,0:T(8,128)(2,1)} %down_ref.1, bf16[16,1024]{1,0:T(8,128)(2,1)} %up_ref.1, bf16[384,1024]{1,0:T(8,128)(2,1)} %pass_hbm.1, s32[384,128]{1,0:T(8,128)} %bitcast.3), custom_call_target="tpu_custom_call" | custom-call | tf_op jit(solution)/shard_map/contrastive/pallas_call | solution.py:525
  84.6 2.8 %finish.1 = (f32[1,1]{1,0:T(1,128)}, f32[16,1024]{1,0:T(8,128)}, f32[16,1024]{1,0:T(8,128)}, bf16[384,1024]{1,0:T(8,128)(2,1)}) custom-call(f32[1,1]{1,0:T(1,128)} %get-tuple-element.11.loss_in, f32[2,128,128]{2,1,0:T(8,128)} %get-tuple-element.12.pieces_ref, bf16[384,1024]{1,0:T(8,128)(2,1)} %get-tuple-element.13.table_in), custom_call_target="tpu_custom_call" | custom-call | tf_op jit(solution)/shard_map/finish/pallas_call | solution.py:566

commit v3 on v2

v3 whole, which is shorter than its diff:
```python
import functools
import math

import jax
import jax.numpy as jnp
from jax import lax
from jax.experimental import pallas as pl
from jax.experimental.pallas import tpu as pltpu
from jax.sharding import PartitionSpec as P

SOFTMAX_TEMPER = 0.02
EPSILON = 1e-06
MESH = pl.DeviceIdType.MESH
F32, BF16 = jnp.float32, jnp.bfloat16
SLOTS = 3
NY = NZ = 8
NX = 4
Q = 24
LISTED = 8
RANK = 16
ROWS = 384
WIDTH = 1024
HALF = WIDTH // 2
TALL, SHORT = 16, 8
DEVS = 2 * NY * NZ
CHIPS = NY * NZ
GROUP = 16 * TALL
VOFF = SLOTS * Q
G_LANE, LOSS_LANE = 120, 121
TINY = 2.0**-80
NEG = -1e38


def nn(a, b):
    return lax.dot_general(a, b, (((1,), (0,)), ((), ())), preferred_element_type=F32)


def nt(a, b):
    return lax.dot_general(a, b, (((1,), (1,)), ((), ())), preferred_element_type=F32)


def tn(a, b):
    return lax.dot_general(a, b, (((0,), (0,)), ((), ())), preferred_element_type=F32)


def exact(dims, a, b):
    return lax.dot_general(a, b, (dims, ((), ())), preferred_element_type=F32, precision=lax.Precision.HIGHEST)


def split(x, parts):
    out = []
    for _ in range(parts):
        top = x.astype(BF16)
        out.append(top)
        x = x - top.astype(F32)
    return out


def iota(shape, dim):
    return lax.broadcasted_iota(jnp.int32, shape, dim)


def kernel(
    ids_hbm, hidden_hbm, down_hbm, up_hbm, pass_hbm, storage_hbm,
    loss_ref, pieces_ref, table_hbm,
    ids_ref, hidden_ref, down_ref, up_ref, hbuf, xb1, xb2, locs, lists, pick, picked, slots, flags, losses, folds, diag, rsx, part, summed, got, back, wrec,
    cand, cand_out, cand_all, piece_out, piece_in, piece_sum, final, mixed_ref, pass_ref, storage_ref, table_ref,
    e1_sem, e2_sem, l_sem, lz_sem, ly_sem, ring_sem, guest_sem, flag_sem, cand_sem, loss_sem, rsx_sem, got_sem, w_sem, rs_sem, ag_sem,
    send_sem, small_sem, load_sem,
):
    me, mp = lax.axis_index("dp"), lax.axis_index("mp")
    core, chip_me = lax.rem(me, 2), me // 2
    y, z = chip_me // NZ, lax.rem(chip_me, NZ)

    def dev(yy, zz, c):
        return ((lax.rem(yy + NY, NY) * NZ + lax.rem(zz + NZ, NZ)) * 2 + c, mp)

    def push(src, dst, ssem, rsem, target):
        pltpu.make_async_remote_copy(
            src_ref=src, dst_ref=dst, send_sem=ssem, recv_sem=rsem, device_id=target, device_id_type=MESH
        ).start()

    def take(ref, sem):
        pltpu.make_async_copy(ref, ref, sem).wait()

    sibling = (chip_me * 2 + 1 - core, mp)

    sa, sb = NZ - (NZ - 1) * core, 1 + (NZ - 1) * core
    a = jnp.where(core == 0, y, z)
    b = jnp.where(core == 0, z, y)

    def line_dev(o):
        return (lax.rem(a + o + NY, NY) * sa + b * sb) * 2 + core

    def cross_dev(o):
        return (a * sa + lax.rem(b + o + NY, NY) * sb) * 2 + core

    loads = [
        pltpu.make_async_copy(src, dst, load_sem.at[i])
        for i, (src, dst) in enumerate((
            (hidden_hbm, hidden_ref), (up_hbm, up_ref), (down_hbm, down_ref),
            (pass_hbm, pass_ref), (storage_hbm, storage_ref), (ids_hbm, ids_ref),
        ))
    ]
    loads[0].start()

    bar = pltpu.get_barrier_semaphore()
    for o in (4, 3, 5, 2, 6, 1, 7):
        pl.semaphore_signal(bar, inc=1, device_id=(line_dev(o), mp), device_id_type=MESH)
        pl.semaphore_signal(bar, inc=1, device_id=(cross_dev(o), mp), device_id_type=MESH)
    pl.semaphore_signal(bar, inc=1, device_id=sibling, device_id_type=MESH)
    for i in range(1, NX):
        pl.semaphore_signal(bar, inc=1, device_id=(me, lax.rem(mp + i, NX)), device_id_type=MESH)

    for cp in loads[1:]:
        cp.start()
    loads[0].wait()
    hid32 = hidden_ref[...].astype(F32)
    hbuf[chip_me, :, 0:WIDTH] = hid32[0:TALL].astype(BF16)
    folded = jnp.concatenate([hid32[TALL:Q, 0:HALF], hid32[TALL:Q, HALF:WIDTH]], axis=0)
    hbuf[chip_me, :, WIDTH : WIDTH + HALF] = folded.astype(BF16)
    pl.semaphore_wait(bar, NY - 1 + NZ - 1 + 1 + NX - 1)

    def chip_of(aa, bb):
        return lax.rem(aa + 2 * NY, NY) * sa + lax.rem(bb + 2 * NY, NY) * sb

    def pass_on(ci, target):
        push(hbuf.at[ci], hbuf.at[ci], send_sem, ring_sem.at[ci], (target, mp))

    for o in (-1, 1, -2, 2, -3, 3, 4):
        pass_on(chip_me, line_dev(o))
    ahead, behind = cross_dev(1), cross_dev(-1)
    offsets = (0, 1, -1, 2, -2, 3, -3, 4)

    def event(t, k):
        if t == 0:
            ci = chip_of(a + offsets[k], b)
            if k > 0:
                take(hbuf.at[ci], ring_sem.at[ci])
            pass_on(ci, ahead)
            pass_on(ci, behind)
            return
        for d in (1, -1):
            last = 4 if (k % 2 == 0) == (d > 0) else 3
            if t <= last:
                ci = chip_of(a + offsets[k], b - d * t)
                take(hbuf.at[ci], ring_sem.at[ci])
                if t < last:
                    pass_on(ci, ahead if d > 0 else behind)

    events = sorted(((t, k) for t in range(5) for k in range(NY)), key=lambda e: (e[0] == 4, 4 * e[0] + e[1]))

    def ring(first, last):
        for t, k in events[first:last]:
            event(t, k)

    loads[1].wait()
    loads[2].wait()
    up32 = up_ref[...].astype(F32)
    left = jnp.concatenate([hid32, up32], axis=0).astype(BF16)
    right = jnp.concatenate([down_ref[...].astype(F32), up32, jnp.zeros((96, WIDTH), F32)], axis=0).astype(BF16)
    prod = nt(left, right)

    loads[3].wait()
    biggest = jnp.max(jnp.max(jnp.abs(pass_ref[...].astype(F32)), axis=0, keepdims=True), axis=1, keepdims=True)
    lane40, row40 = iota((40, 128), 1), iota((40, 128), 0)
    xb1[mp] = jnp.where((lane40 == 40) & (row40 == 0), biggest, prod)
    for i in range(1, NX):
        push(xb1.at[mp], xb1.at[mp], small_sem.at[1], e1_sem, (me, lax.rem(mp + i, NX)))

    loads[4].wait()
    loads[5].wait()
    lane1 = iota((1, 128), 1)
    for j in range(Q * LISTED):
        pid = ids_ref[j % LISTED, j // LISTED]
        row = storage_ref[pl.ds(pid // 128, 1), :]
        locs[pl.ds(j, 1), :] = jnp.where(lane1 == lax.rem(pid, 128), row, 0).astype(F32)
    located = jnp.sum(locs[...], axis=1, keepdims=True)
    located = jnp.concatenate([located, jnp.full((64, 1), 1e6, F32)], axis=0)
    r256, l256 = iota((256, 256), 0), iota((256, 256), 1)
    as_row = jnp.sum(jnp.where(r256 == l256, located, 0.0), axis=0, keepdims=True)
    lists[0, core, pl.ds(chip_me, 1), :] = as_row[:, 0:128]
    lists[1, core, pl.ds(chip_me, 1), :] = as_row[:, 128:256]
    own_list = lists.at[:, core, pl.ds(chip_me, 1), :]
    push(own_list, own_list, small_sem.at[2], l_sem, sibling)

    take(lists.at[:, 0, pl.ds(0, 1), :], l_sem)

    def some_lists(first, n):
        return lists.at[:, :, pl.ds(pl.multiple_of(first, n), n), :]

    for o in (4, 3, 5, 2, 6, 1, 7):
        r = some_lists(chip_me, 1)
        push(r, r, small_sem.at[4], lz_sem.at[z], dev(y, z + o, core))

    def lists_on():
        def each(i, c):
            zz = lax.rem(z + i, NZ)
            take(some_lists(y * NZ + zz, 1), lz_sem.at[zz])
            return c
        lax.fori_loop(1, NZ, each, 0)
        for o in (4, 3, 5, 2, 6, 1, 7):
            r = some_lists(y * NZ, NZ)
            push(r, r, small_sem.at[5], ly_sem.at[y], dev(y + o, z, core))

    def lists_done():
        def each(i, c):
            yy = lax.rem(y + i, NY)
            take(some_lists(yy * NZ, NZ), ly_sem.at[yy])
            return c
        lax.fori_loop(1, NY, each, 0)

    ring(0, 8)

    take(xb1.at[pl.ds(0, NX - 1)], e1_sem)
    tot = xb1[0] + xb1[1] + xb1[2] + xb1[3]
    most = jnp.maximum(jnp.maximum(xb1[0], xb1[1]), jnp.maximum(xb1[2], xb1[3]))
    most = jnp.max(jnp.where((lane40 == 40) & (row40 == 0), most, 0.0))
    shrink = jnp.where(most > 2.0**40, TINY, 1.0)
    low_half = tot[0:Q, 0:RANK].astype(BF16)
    rolled = pltpu.roll(tot, 128 - RANK, 1)
    hid_up, gram = rolled[0:Q, 0:RANK], rolled[Q : Q + RANK, 0:RANK]
    mixed = hid32 + nn(low_half, up_ref[...])
    mixed_ref[...] = mixed
    xb2[mp] = jnp.broadcast_to(jnp.sum(mixed * mixed, axis=1, keepdims=True), (Q, 128))
    for i in range(1, NX):
        push(xb2.at[mp], xb2.at[mp], small_sem.at[3], e2_sem, (me, lax.rem(mp + i, NX)))

    flags[core] = jnp.full((8, 128), shrink, F32)
    push(flags.at[core], flags.at[core], small_sem.at[11], flag_sem, sibling)

    ring(8, 14)
    lists_on()
    ring(14, 24)

    take(xb2.at[pl.ds(0, NX - 1)], e2_sem)
    inv_norm = lax.rsqrt((xb2[0] + xb2[1] + xb2[2] + xb2[3]) / (WIDTH * NX) + EPSILON)

    ring(24, 32)
    lists_done()

    wanted = jnp.concatenate([lists[0].reshape(DEVS, 128), lists[1].reshape(DEVS, 128)], axis=1) - (me * ROWS).astype(F32)
    here = (wanted >= 0.0) & (wanted < ROWS)
    earlier = nn(here.astype(F32).astype(BF16), (r256 < l256).astype(F32).astype(BF16))
    rows_iota = iota((DEVS, ROWS), 1).astype(F32)
    for s in range(SLOTS):
        col = jnp.sum(jnp.where(here & (earlier == s), wanted + 1.0, 0.0), axis=1, keepdims=True) - 1.0
        pk = (rows_iota == col).astype(F32).astype(BF16)
        pick[s] = pk
        picked[s] = (nn(pk, pass_ref[...]) * shrink).astype(BF16)
        f_lane = iota((GROUP, 128), 1) - s * Q
        f_row = iota((GROUP, 128), 0)
        folds[0, s] = (f_lane == lax.rem(f_row, TALL)).astype(F32).astype(BF16)
        folds[1, s] = (f_lane == TALL + lax.rem(f_row, SHORT)).astype(F32).astype(BF16)
    guests = pl.ds(pl.multiple_of((1 - core) * CHIPS, CHIPS), CHIPS)
    push(picked.at[:, guests, :], slots.at[core], small_sem.at[0], guest_sem, sibling)
    for s in range(SLOTS):
        slots[core, s] = picked[s, pl.ds(pl.multiple_of(core * CHIPS, CHIPS), CHIPS), :]

    owner = jnp.floor((located + 0.5) * (1.0 / ROWS))
    owner_chip = jnp.floor(owner * 0.5)
    owner = (owner - 2.0 * owner_chip) * CHIPS + owner_chip
    hold = (iota((256, 128), 1).astype(F32) == owner).astype(F32)
    hold_b = hold.astype(BF16)
    rank = jnp.sum(hold * nn((r256 > l256).astype(F32).astype(BF16), hold_b), axis=1, keepdims=True)
    count = tn(hold_b, jnp.ones((256, 128), BF16))
    l_col = iota((256, 128), 1)
    pos_at = (iota((256, 128), 0) == LISTED * lax.rem(l_col, Q)) & (rank == (l_col // Q).astype(F32)) & (l_col < VOFF)
    positive = tn(hold_b, pos_at.astype(F32).astype(BF16))
    lane = iota((DEVS, 128), 1)
    valid = (count > (lane // Q).astype(F32)) & (lane < VOFF)

    row128 = iota((128, RANK), 0)
    at_rank = ((row128 >= VOFF) & (row128 < VOFF + SLOTS * RANK) & (lax.rem(row128 - VOFF + 128 * RANK, RANK) == iota((128, RANK), 1)))
    at_rank = at_rank.astype(F32)
    at_query = ((iota((Q, 128), 1) < VOFF) & (lax.rem(iota((Q, 128), 1), Q) == iota((Q, 128), 0))).astype(F32)
    spread = nn(nt(at_rank.astype(BF16), low_half).astype(BF16), at_query.astype(BF16))
    row_a, lane_a = iota((128, 128), 0), iota((128, 128), 1)
    same_slot = ((row_a + 128 * RANK - VOFF) // RANK - 128) == lane_a // Q
    spread = jnp.where(same_slot, spread, 0.0).astype(BF16)
    inv_lane = jnp.sum(inv_norm * at_query, axis=0, keepdims=True)

    ring(32, 36)

    take(slots.at[0], guest_sem)
    take(flags.at[0], flag_sem)

    def slot_rows(s):
        return slots[:, s].reshape(DEVS, WIDTH)

    def up_lanes(s):
        return jnp.concatenate(
            [jnp.zeros((VOFF + s * RANK, WIDTH), F32), up32, jnp.zeros((128 - VOFF - (s + 1) * RANK, WIDTH), F32)], axis=0
        ).astype(BF16)

    part_pu = jnp.zeros((DEVS, 128), F32)
    for s in range(SLOTS):
        part_pu = part_pu + nt(slot_rows(s), up_lanes(s))

    ring(36, 40)

    SG = 2 * SLOTS * 16
    block_t = lax.rem(iota((TALL, SG), 1), 16)
    block_s = lax.rem(iota((SHORT, SG), 1), 16)

    def tall(g):
        return hbuf[pl.ds(g * 16, 16), :, 0:WIDTH].reshape(GROUP, WIDTH)

    def short(g):
        return hbuf[pl.ds(g * 16, 16), :, WIDTH : WIDTH + HALF].reshape(GROUP, HALF)

    for g in range(CHIPS // 16):
        rows = pl.ds(g * 16, 16)
        s_g = jnp.concatenate([slots[h, s, rows, :] for h in (0, 1) for s in range(SLOTS)], axis=0)
        d = nt(tall(g), s_g)
        d_lo, d_hi = nt(short(g), s_g[:, 0:HALF]), nt(short(g), s_g[:, HALF:WIDTH])
        e, f = jnp.zeros((TALL, SG), F32), jnp.zeros((SHORT, SG), F32)
        for r in range(16):
            at = r * TALL
            e = e + jnp.where(block_t == r, d[at : at + TALL, :], 0.0)
            f = f + jnp.where(block_s == r, d_lo[at : at + SHORT, :] + d_hi[at + SHORT : at + TALL, :], 0.0)
        e = jnp.concatenate([e, f], axis=0)
        e = jnp.concatenate([e, jnp.zeros((Q, 128 - SG), F32)], axis=1)
        e = jnp.transpose(jnp.concatenate([e, jnp.zeros((128 - Q, 128), F32)], axis=0))
        for h in (0, 1):
            at = h * SLOTS * 16
            one = e[at : at + 16, :] + pltpu.roll(e[at + 16 : at + 32, :], Q, 1) + pltpu.roll(e[at + 32 : at + 48, :], 2 * Q, 1)
            one = one + part_pu[h * CHIPS + g * 16 : h * CHIPS + (g + 1) * 16, :]
            part[h, rows, :] = one + jnp.where(lane[0:16] == G_LANE, flags[h, 0:1, :] * (1.0 / NX), 0.0)

    quarter = CHIPS // NX

    def q_rows(k):
        return part.at[:, pl.ds(pl.multiple_of(k * quarter, quarter), quarter), :]

    for i in range(1, NX):
        k = lax.rem(mp + i, NX)
        push(q_rows(k), rsx.at[mp], small_sem.at[6], rsx_sem, (me, k))
    rsx[mp] = part[:, pl.ds(pl.multiple_of(mp * quarter, quarter), quarter), :]
    take(rsx.at[pl.ds(0, NX - 1)], rsx_sem)
    summed[...] = rsx[0] + rsx[1] + rsx[2] + rsx[3]

    def swing(m):
        return ((8 - m) // 2) * (2 * lax.rem(m, 2) - 1)

    def far_first(m):
        return ((8 - m) // 2) * (1 if m % 2 else -1)

    def to_all(send, both):
        inner = [lax.rem(z + far_first(n) + NZ, NZ) for n in range(NZ)]
        cores = (1 - core, core) if both else (core,)

        def far_rows(m, carry):
            base = lax.rem(y + swing(m) + NY, NY) * NZ
            for n in inner:
                for c in cores:
                    send(base + n, c)
            return carry

        lax.fori_loop(0, NY - 1, far_rows, 0)
        for i, n in enumerate(inner):
            for c in cores[: len(cores) if i < NZ - 1 else len(cores) - 1]:
                send(y * NZ + n, c)

    def row_of(ref, chip):
        return ref.at[:, pl.ds(chip, 1), :]

    home = (chip_me // quarter) == mp
    others = [lax.rem(mp + dk, NX) for dk in (2, 1, 3)]

    def give(m, c):
        first = lax.rem(z + swing(m) + NZ, NZ)
        for j in (first, first + NZ):
            chip = mp * quarter + j
            for k in others:
                push(row_of(summed, j), row_of(got, chip_me), small_sem.at[7], got_sem, (chip * 2 + core, k))

            @pl.when(chip != chip_me)
            def _():
                push(row_of(summed, j), row_of(got, chip_me), small_sem.at[7], got_sem, (chip * 2 + core, mp))
        return c

    lax.fori_loop(0, NZ, give, 0)

    @pl.when(home)
    def _():
        pltpu.make_async_copy(row_of(summed, lax.rem(chip_me, quarter)), row_of(got, chip_me), got_sem).start()

    take(got, got_sem)

    g = got[...].reshape(DEVS, 128)
    unshrink = jnp.sum(jnp.where(lane == G_LANE, g, 0.0), axis=1, keepdims=True)
    unshrink = jnp.where(unshrink < 0.5, 1.0 / TINY, 1.0)
    ranks = jnp.where((lane >= VOFF) & (lane < VOFF + SLOTS * RANK), g, 0.0)
    raw = g
    for piece in split(ranks, 3):
        raw = raw + nn(piece, spread)
    raw = jnp.where(valid & (inv_lane > 0.0), raw * inv_lane * unshrink, 0.0)
    scale = 1.0 / (SOFTMAX_TEMPER * math.sqrt(WIDTH * NX))
    scores = jnp.where(valid, raw * scale, NEG)

    def over_slots(x, op, fill):
        x0 = op(op(x, pltpu.roll(x, 128 - Q, 1)), pltpu.roll(x, 128 - 2 * Q, 1))
        return jnp.where(lane1 < Q, x0, jnp.where(lane1 < 2 * Q, pltpu.roll(x0, Q, 1), jnp.where(lane1 < 3 * Q, pltpu.roll(x0, 2 * Q, 1), fill)))

    top = over_slots(jnp.max(scores, axis=0, keepdims=True), jnp.maximum, 0.0)
    expo = jnp.where(valid, jnp.exp(scores - top), 0.0)
    total = over_slots(jnp.sum(expo, axis=0, keepdims=True), jnp.add, 1.0)
    own = over_slots(jnp.sum(jnp.where(positive > 0.5, scores, 0.0), axis=0, keepdims=True), jnp.add, 0.0)
    loss = jnp.sum(jnp.where(lane1 < Q, jnp.log(total) + top - own, 0.0), axis=1, keepdims=True)
    weights = jnp.where(valid, (expo / total - positive) * scale, 0.0)
    tangent = over_slots(jnp.sum(weights * raw, axis=0, keepdims=True), jnp.add, 0.0) / (WIDTH * NX)
    w2 = weights * inv_lane
    v = jnp.zeros((DEVS, 128), F32)
    for piece in split(w2, 3):
        v = v + nt(piece, spread)
    back[...] = (w2 + v + jnp.where(lane == LOSS_LANE, loss, 0.0)).reshape(2, CHIPS, 128)

    to_all(lambda chip, c: push(row_of(back, chip), row_of(wrec, chip_me), small_sem.at[8], w_sem, (chip * 2 + c, mp)), False)
    pltpu.make_async_copy(row_of(back, chip_me), row_of(wrec, chip_me), w_sem).start()

    z_all = exact(((0,), (0,)), weights, ranks * unshrink)
    z_all = jnp.where(lane_a >= VOFF, z_all, 0.0)
    same_t = ((lane_a + 128 * RANK - VOFF) // RANK - 128) == row_a // Q
    z_all = jnp.where(same_t, z_all, 0.0)
    w_pu = exact(((1,), (0,)), exact(((1,), (0,)), at_query, z_all), at_rank)
    inv_col = inv_norm[:, 0:1]
    q_up = inv_col * (hid_up + exact(((1,), (0,)), low_half.astype(F32), gram))
    tan_col = jnp.sum(jnp.where((iota((Q, 128), 1) < Q), at_query, 0.0) * tangent, axis=1, keepdims=True)
    low_grad = (inv_col * (w_pu - tan_col * q_up)).astype(BF16)
    ga = tn(low_grad, hidden_ref[...])
    pulled = (mixed_ref[...] * (inv_col * inv_col * tan_col)).astype(BF16)
    gb = -tn(low_half, pulled)

    take(wrec, w_sem)
    w = wrec[...].reshape(DEVS, 128)
    lost = jnp.where((lane == LOSS_LANE) & (iota((DEVS, 128), 0) < CHIPS), w, 0.0)
    losses[core] = jnp.broadcast_to(jnp.sum(jnp.sum(lost, axis=0, keepdims=True), axis=1, keepdims=True), (8, 128))
    push(losses.at[core], losses.at[core], small_sem.at[13], loss_sem, sibling)
    w_t = jnp.transpose(w) * jnp.where(lane1 < CHIPS, 1.0 / flags[0, 0:1, :], 1.0 / flags[1, 0:1, :])
    for s in range(SLOTS):
        for piece in split(w_t[VOFF + s * RANK : VOFF + (s + 1) * RANK, :], 2):
            gb = gb + nn(piece, slot_rows(s))
    for j in range(WIDTH // 128):
        piece_out[0, pl.ds(j * RANK, RANK), :] = ga[:, j * 128 : (j + 1) * 128]
        piece_out[1, pl.ds(j * RANK, RANK), :] = gb[:, j * 128 : (j + 1) * 128]

    to_all(lambda chip, c: push(row_of(piece_out, chip * 2 + c), row_of(piece_in, me), small_sem.at[9], rs_sem, (chip * 2 + c, mp)), True)
    pltpu.make_async_copy(piece_out.at[:, pl.ds(me, 1), :], piece_in.at[:, pl.ds(me, 1), :], rs_sem).start()

    hi, lo = split(w, 2)
    d_lane = iota((DEVS, GROUP), 1)
    wide = (d_lane // TALL) == lax.rem(iota((DEVS, GROUP), 0), 16)
    first_half = lax.rem(d_lane // SHORT, 2) == 0
    for s in range(SLOTS):
        for i, piece in enumerate((hi, lo)):
            diag[0, i, s] = jnp.where(wide, nt(piece, folds[0, s]), 0.0).astype(BF16)
            low8 = jnp.where(wide, nt(piece, folds[1, s]), 0.0)
            diag[1, i, s] = jnp.where(first_half, low8, 0.0).astype(BF16)
            diag[2, i, s] = jnp.where(first_half, 0.0, low8).astype(BF16)

    def candidates(g_, c):
        rows = pl.ds(pl.multiple_of(g_ * 16, 16), 16)
        d0, d1, d2 = (
            jnp.concatenate(
                [diag[n, i, s, pl.ds(pl.multiple_of(h * CHIPS + g_ * 16, 16), 16), :] for i in (0, 1) for h in (0, 1) for s in range(SLOTS)],
                axis=0,
            )
            for n in range(3)
        )
        o = nn(d0, tall(g_)) + jnp.concatenate([nn(d1, short(g_)), nn(d2, short(g_))], axis=1)
        o = o[0:SG, :] + o[SG : 2 * SG, :]
        for h in (0, 1):
            for s in range(SLOTS):
                at = (h * SLOTS + s) * 16
                cand[h, s, rows, :] = o[at : at + 16, :]
        return c

    lax.fori_loop(0, CHIPS // 16, candidates, 0)
    for s in range(SLOTS):
        up_at = up_lanes(s)
        cg = cand[:, s].reshape(DEVS, WIDTH) + nn(hi, up_at) + nn(lo, up_at)
        cand_out[:, s] = cg.astype(BF16).reshape(2, CHIPS, WIDTH)
    push(cand_out.at[1 - core], cand_all.at[core], small_sem.at[12], cand_sem, sibling)
    cand_all[core] = cand_out[core]

    take(piece_in, rs_sem)
    piece_sum[...] = jnp.sum(piece_in[...], axis=1, keepdims=True)
    final[:, pl.ds(me, 1), :] = piece_sum[...]

    to_all(lambda chip, c: push(piece_sum, row_of(final, me), small_sem.at[10], ag_sem, (chip * 2 + c, mp)), True)
    take(cand_all.at[0], cand_sem)
    table = jnp.zeros((ROWS, WIDTH), F32)
    for s in range(SLOTS):
        table = table + tn(pick[s], cand_all[:, s].reshape(DEVS, WIDTH))
    table_ref[...] = table.astype(BF16)
    table_out = pltpu.make_async_copy(table_ref, table_hbm, load_sem.at[6])
    table_out.start()

    take(final.at[:, pl.ds(0, DEVS - 1), :], ag_sem)
    pieces_ref[...] = final[...]
    take(losses.at[0], loss_sem)
    loss_ref[...] = (losses[0, 0:1, 0:1] + losses[1, 0:1, 0:1]) / (DEVS * Q)
    table_out.wait()

    take(hbuf.at[pl.ds(0, CHIPS - 1)], send_sem)
    take(picked.at[:, pl.ds(0, CHIPS), :], small_sem.at[0])
    take(xb1.at[pl.ds(0, NX - 1)], small_sem.at[1])
    take(lists.at[:, 0, pl.ds(0, 1), :], small_sem.at[2])
    take(xb2.at[pl.ds(0, NX - 1)], small_sem.at[3])
    take(lists.at[:, :, pl.ds(0, NZ - 1), :], small_sem.at[4])
    take(lists.at[:, :, pl.ds(0, NZ * (NY - 1)), :], small_sem.at[5])
    take(rsx.at[pl.ds(0, NX - 1)], small_sem.at[6])
    @pl.when(home)
    def _():
        take(got.at[:, pl.ds(0, CHIPS - 1), :], small_sem.at[7])

    @pl.when(jnp.logical_not(home))
    def _():
        take(got, small_sem.at[7])

    take(wrec.at[:, pl.ds(0, CHIPS - 1), :], small_sem.at[8])
    take(piece_in.at[:, pl.ds(0, DEVS - 1), :], small_sem.at[9])
    take(final.at[:, pl.ds(0, DEVS - 1), :], small_sem.at[10])
    take(flags.at[0], small_sem.at[11])
    take(losses.at[0], small_sem.at[13])
    take(cand_out.at[0], small_sem.at[12])


def finish(loss_in, pieces_ref, table_in, loss_ref, ga_ref, gb_ref, table_out, buf, in_sem, out_sem):
    step = ROWS // 4
    ins = [
        pltpu.make_async_copy(table_in.at[pl.ds(i * step, step), :], buf.at[pl.ds(i * step, step), :], in_sem.at[i])
        for i in range(4)
    ]
    outs = [
        pltpu.make_async_copy(buf.at[pl.ds(i * step, step), :], table_out.at[pl.ds(i * step, step), :], out_sem.at[i])
        for i in range(4)
    ]
    for cp in ins:
        cp.start()
    loss_ref[...] = loss_in[...]
    for j in range(WIDTH // 128):
        ga_ref[:, pl.ds(j * 128, 128)] = pieces_ref[0, pl.ds(j * RANK, RANK), :]
        gb_ref[:, pl.ds(j * 128, 128)] = pieces_ref[1, pl.ds(j * RANK, RANK), :]
    for cin, cout in zip(ins, outs, strict=True):
        cin.wait()
        cout.start()
    for cp in outs:
        cp.wait()


def shards(hidden, down, up, passages, ids, storage):
    vm, hbm = pl.BlockSpec(memory_space=pltpu.VMEM), pl.BlockSpec(memory_space=pl.ANY)
    dma = pltpu.SemaphoreType.DMA
    shape = jax.ShapeDtypeStruct
    loss, pieces, table = pl.pallas_call(
        kernel,
        out_shape=(shape((1, 1), F32), shape((2, DEVS, 128), F32), shape((ROWS, WIDTH), BF16)),
        in_specs=[hbm] * 6,
        out_specs=(vm, vm, hbm),
        scratch_shapes=[
            pltpu.SMEM((LISTED, Q), jnp.int32),
            pltpu.VMEM((Q, WIDTH), BF16),
            pltpu.VMEM((RANK, WIDTH), BF16),
            pltpu.VMEM((RANK, WIDTH), BF16),
            pltpu.VMEM((CHIPS, TALL, WIDTH + HALF), BF16),
            pltpu.VMEM((NX, 40, 128), F32),
            pltpu.VMEM((NX, Q, 128), F32),
            pltpu.VMEM((Q * LISTED, 128), F32),
            pltpu.VMEM((2, 2, CHIPS, 128), F32),
            pltpu.VMEM((SLOTS, DEVS, ROWS), BF16),
            pltpu.VMEM((SLOTS, DEVS, WIDTH), BF16),
            pltpu.VMEM((2, SLOTS, CHIPS, WIDTH), BF16),
            pltpu.VMEM((2, 8, 128), F32),
            pltpu.VMEM((2, 8, 128), F32),
            pltpu.VMEM((2, SLOTS, GROUP, 128), BF16),
            pltpu.VMEM((3, 2, SLOTS, DEVS, GROUP), BF16),
            pltpu.VMEM((NX, 2, CHIPS // NX, 128), F32),
            pltpu.VMEM((2, CHIPS, 128), F32),
            pltpu.VMEM((2, CHIPS // NX, 128), F32),
            pltpu.VMEM((2, CHIPS, 128), F32),
            pltpu.VMEM((2, CHIPS, 128), F32),
            pltpu.VMEM((2, CHIPS, 128), F32),
            pltpu.VMEM((2, SLOTS, CHIPS, WIDTH), F32),
            pltpu.VMEM((2, SLOTS, CHIPS, WIDTH), BF16),
            pltpu.VMEM((2, SLOTS, CHIPS, WIDTH), BF16),
            pltpu.VMEM((2, DEVS, 128), F32),
            pltpu.VMEM((2, DEVS, 128), F32),
            pltpu.VMEM((2, 1, 128), F32),
            pltpu.VMEM((2, DEVS, 128), F32),
            pltpu.VMEM((Q, WIDTH), F32),
            pltpu.VMEM((ROWS, WIDTH), BF16),
            pltpu.VMEM((ROWS, 128), jnp.int32),
            pltpu.VMEM((ROWS, WIDTH), BF16),
            dma, dma, dma,
            dma((NZ,)), dma((NY,)),
            dma((CHIPS,)), dma, dma, dma, dma,
            dma, dma, dma, dma, dma,
            dma, dma((14,)), dma((7,)),
        ],
        compiler_params=pltpu.CompilerParams(collective_id=0, has_side_effects=True, vmem_limit_bytes=56 << 20),
        name="contrastive",
    )(ids.T, hidden, down, up, passages, storage.reshape(ROWS, 128))
    loss, ga, gb, table = pl.pallas_call(
        finish,
        out_shape=(shape((1, 1), F32), shape((RANK, WIDTH), F32), shape((RANK, WIDTH), F32), shape((ROWS, WIDTH), BF16)),
        in_specs=[vm, vm, hbm],
        out_specs=(vm, vm, vm, hbm),
        scratch_shapes=[pltpu.VMEM((ROWS, WIDTH), BF16), dma((4,)), dma((4,))],
        name="finish",
    )(loss, pieces, table)
    return loss.reshape(()), ga, gb, table


def solution(mesh):
    return jax.shard_map(
        shards,
        mesh=mesh,
        in_specs=(P("dp", "mp"), P(None, "mp"), P(None, "mp"), P("dp", "mp"), P("dp", None), P()),
        out_specs=(P(), P(None, "mp"), P(None, "mp"), P("dp", "mp")),
        check_vma=False,
    )
```

time: 87.6 us -> 84.5 us (0.965)
  Pallas kernels: 86.8 us -> 83.7 us
    pallas_call x1, Pallas kernels: 84 us -> 79.5 us  [shards(): pl.pallas_call(kernel, out_shape=(shape((1, 1), F32), shape((2, DEVS, 128...]
    pallas_call x1, Pallas kernels: 2.78 us -> 4.14 us  [shards(): pl.pallas_call(finish, out_shape=(shape((1, 1), F32), shape((RANK, WIDTH)...]
where the time goes in v3:
time: 84.5 us; the launch traced here: 84.3 us
  Pallas kernels  83.7 us (99%)
    pallas_call x1, Pallas kernels, shards(): pl.pallas_call(kernel, out_shape=(shape((1, 1), F32), shape((2, DEVS, 128...  79.5 us
    pallas_call x1, Pallas kernels, shards(): pl.pallas_call(finish, out_shape=(shape((1, 1), F32), shape((RANK, WIDTH)...  4.14 us

profile of v3, /device:TPU:1, one launch (start us, length us, event | category | flops | bytes accessed | tf_op | source)
XLA Modules:
  0.0 84.3 jit_solution(3381411056930855455)
XLA Ops:
  0.6 79.5 %contrastive.1 = (f32[1,1]{1,0:T(1,128)}, f32[2,128,128]{2,1,0:T(8,128)}, bf16[384,1024]{1,0:T(8,128)(2,1)}) custom-call(s32[8,24]{1,0:T(8,128)} %bitcast.4, bf16[24,1024]{1,0:T(8,128)(2,1)} %hidden_hbm.1, bf16[16,1024]{1,0:T(8,128)(2,1)} %down_hbm.1, bf16[16,1024]{1,0:T(8,128)(2,1)} %up_hbm.1, bf16[384,1024]{1,0:T(8,128)(2,1)} %pass_hbm.1, s32[384,128]{1,0:T(8,128)} %bitcast.3), custom_call_target="tpu_custom_call" | custom-call | tf_op jit(solution)/shard_map/contrastive/pallas_call | solution.py:557
  80.2 4.1 %finish.1 = (f32[1,1]{1,0:T(1,128)}, f32[16,1024]{1,0:T(8,128)}, f32[16,1024]{1,0:T(8,128)}, bf16[384,1024]{1,0:T(8,128)(2,1)}) custom-call(f32[1,1]{1,0:T(1,128)} %get-tuple-element.11.loss_in, f32[2,128,128]{2,1,0:T(8,128)} %get-tuple-element.12.pieces_ref, bf16[384,1024]{1,0:T(8,128)(2,1)} %get-tuple-element.13.table_in), custom_call_target="tpu_custom_call" | custom-call | tf_op jit(solution)/shard_map/finish/pallas_call | solution.py:605

commit v4 on v3

--- a/solution.py
+++ b/solution.py
@@ -148,7 +148,7 @@
                 if t < last:
                     pass_on(ci, ahead if d > 0 else behind)
 
-    events = sorted(((t, k) for t in range(5) for k in range(NY)), key=lambda e: (e[0] == 4, 4 * e[0] + e[1]))
+    events = sorted(((t, k) for t in range(5) for k in range(NY)), key=lambda e: (e[0] == 4, 8 * e[0] + e[1]))
 
     def ring(first, last):
         for t, k in events[first:last]:
@@ -248,39 +248,13 @@
         pk = (rows_iota == col).astype(F32).astype(BF16)
         pick[s] = pk
         picked[s] = (nn(pk, pass_ref[...]) * shrink).astype(BF16)
-        f_lane = iota((GROUP, 128), 1) - s * Q
-        f_row = iota((GROUP, 128), 0)
-        folds[0, s] = (f_lane == lax.rem(f_row, TALL)).astype(F32).astype(BF16)
-        folds[1, s] = (f_lane == TALL + lax.rem(f_row, SHORT)).astype(F32).astype(BF16)
     guests = pl.ds(pl.multiple_of((1 - core) * CHIPS, CHIPS), CHIPS)
     push(picked.at[:, guests, :], slots.at[core], small_sem.at[0], guest_sem, sibling)
     for s in range(SLOTS):
         slots[core, s] = picked[s, pl.ds(pl.multiple_of(core * CHIPS, CHIPS), CHIPS), :]
 
-    owner = jnp.floor((located + 0.5) * (1.0 / ROWS))
-    owner_chip = jnp.floor(owner * 0.5)
-    owner = (owner - 2.0 * owner_chip) * CHIPS + owner_chip
-    hold = (iota((256, 128), 1).astype(F32) == owner).astype(F32)
-    hold_b = hold.astype(BF16)
-    rank = jnp.sum(hold * nn((r256 > l256).astype(F32).astype(BF16), hold_b), axis=1, keepdims=True)
-    count = tn(hold_b, jnp.ones((256, 128), BF16))
-    l_col = iota((256, 128), 1)
-    pos_at = (iota((256, 128), 0) == LISTED * lax.rem(l_col, Q)) & (rank == (l_col // Q).astype(F32)) & (l_col < VOFF)
-    positive = tn(hold_b, pos_at.astype(F32).astype(BF16))
+    ring(32, 36)
     lane = iota((DEVS, 128), 1)
-    valid = (count > (lane // Q).astype(F32)) & (lane < VOFF)
-
-    row128 = iota((128, RANK), 0)
-    at_rank = ((row128 >= VOFF) & (row128 < VOFF + SLOTS * RANK) & (lax.rem(row128 - VOFF + 128 * RANK, RANK) == iota((128, RANK), 1)))
-    at_rank = at_rank.astype(F32)
-    at_query = ((iota((Q, 128), 1) < VOFF) & (lax.rem(iota((Q, 128), 1), Q) == iota((Q, 128), 0))).astype(F32)
-    spread = nn(nt(at_rank.astype(BF16), low_half).astype(BF16), at_query.astype(BF16))
-    row_a, lane_a = iota((128, 128), 0), iota((128, 128), 1)
-    same_slot = ((row_a + 128 * RANK - VOFF) // RANK - 128) == lane_a // Q
-    spread = jnp.where(same_slot, spread, 0.0).astype(BF16)
-    inv_lane = jnp.sum(inv_norm * at_query, axis=0, keepdims=True)
-
-    ring(32, 36)
 
     take(slots.at[0], guest_sem)
     take(flags.at[0], flag_sem)
@@ -299,18 +273,23 @@
 
     ring(36, 40)
 
+    quarter = CHIPS // NX
+    for h in (0, 1):
+        shrink_row = jnp.where(lane[0:CHIPS] == G_LANE, flags[h, 0:1, :] * (1.0 / NX), 0.0)
+        part[h] = part_pu[h * CHIPS : (h + 1) * CHIPS, :] + shrink_row
     SG = 2 * SLOTS * 16
     block_t = lax.rem(iota((TALL, SG), 1), 16)
     block_s = lax.rem(iota((SHORT, SG), 1), 16)
 
     def tall(g):
-        return hbuf[pl.ds(g * 16, 16), :, 0:WIDTH].reshape(GROUP, WIDTH)
+        return hbuf[pl.ds(pl.multiple_of(g * 16, 16), 16), :, 0:WIDTH].reshape(GROUP, WIDTH)
 
     def short(g):
-        return hbuf[pl.ds(g * 16, 16), :, WIDTH : WIDTH + HALF].reshape(GROUP, HALF)
-
-    for g in range(CHIPS // 16):
-        rows = pl.ds(g * 16, 16)
+        return hbuf[pl.ds(pl.multiple_of(g * 16, 16), 16), :, WIDTH : WIDTH + HALF].reshape(GROUP, HALF)
+
+    for i in range(1, NX + 1):
+        g = lax.rem(mp + i, NX)
+        rows = pl.ds(pl.multiple_of(g * 16, 16), 16)
         s_g = jnp.concatenate([slots[h, s, rows, :] for h in (0, 1) for s in range(SLOTS)], axis=0)
         d = nt(tall(g), s_g)
         d_lo, d_hi = nt(short(g), s_g[:, 0:HALF]), nt(short(g), s_g[:, HALF:WIDTH])
@@ -325,18 +304,12 @@
         for h in (0, 1):
             at = h * SLOTS * 16
             one = e[at : at + 16, :] + pltpu.roll(e[at + 16 : at + 32, :], Q, 1) + pltpu.roll(e[at + 32 : at + 48, :], 2 * Q, 1)
-            one = one + part_pu[h * CHIPS + g * 16 : h * CHIPS + (g + 1) * 16, :]
-            part[h, rows, :] = one + jnp.where(lane[0:16] == G_LANE, flags[h, 0:1, :] * (1.0 / NX), 0.0)
-
-    quarter = CHIPS // NX
-
-    def q_rows(k):
-        return part.at[:, pl.ds(pl.multiple_of(k * quarter, quarter), quarter), :]
-
-    for i in range(1, NX):
-        k = lax.rem(mp + i, NX)
-        push(q_rows(k), rsx.at[mp], small_sem.at[6], rsx_sem, (me, k))
-    rsx[mp] = part[:, pl.ds(pl.multiple_of(mp * quarter, quarter), quarter), :]
+            part[h, rows, :] = part[h, rows, :] + one
+        if i < NX:
+            push(part.at[:, rows, :], rsx.at[mp], small_sem.at[6], rsx_sem, (me, g))
+        else:
+            rsx[mp] = part[:, rows, :]
+
     take(rsx.at[pl.ds(0, NX - 1)], rsx_sem)
     summed[...] = rsx[0] + rsx[1] + rsx[2] + rsx[3]
 
@@ -386,6 +359,33 @@
     def _():
         pltpu.make_async_copy(row_of(summed, lax.rem(chip_me, quarter)), row_of(got, chip_me), got_sem).start()
 
+    owner = jnp.floor((located + 0.5) * (1.0 / ROWS))
+    owner_chip = jnp.floor(owner * 0.5)
+    owner = (owner - 2.0 * owner_chip) * CHIPS + owner_chip
+    hold = (iota((256, 128), 1).astype(F32) == owner).astype(F32)
+    hold_b = hold.astype(BF16)
+    rank = jnp.sum(hold * nn((r256 > l256).astype(F32).astype(BF16), hold_b), axis=1, keepdims=True)
+    count = tn(hold_b, jnp.ones((256, 128), BF16))
+    l_col = iota((256, 128), 1)
+    pos_at = (iota((256, 128), 0) == LISTED * lax.rem(l_col, Q)) & (rank == (l_col // Q).astype(F32)) & (l_col < VOFF)
+    positive = tn(hold_b, pos_at.astype(F32).astype(BF16))
+    valid = (count > (lane // Q).astype(F32)) & (lane < VOFF)
+
+    row128 = iota((128, RANK), 0)
+    at_rank = ((row128 >= VOFF) & (row128 < VOFF + SLOTS * RANK) & (lax.rem(row128 - VOFF + 128 * RANK, RANK) == iota((128, RANK), 1)))
+    at_rank = at_rank.astype(F32)
+    at_query = ((iota((Q, 128), 1) < VOFF) & (lax.rem(iota((Q, 128), 1), Q) == iota((Q, 128), 0))).astype(F32)
+    spread = nn(nt(at_rank.astype(BF16), low_half).astype(BF16), at_query.astype(BF16))
+    row_a, lane_a = iota((128, 128), 0), iota((128, 128), 1)
+    same_slot = ((row_a + 128 * RANK - VOFF) // RANK - 128) == lane_a // Q
+    spread = jnp.where(same_slot, spread, 0.0).astype(BF16)
+    inv_lane = jnp.sum(inv_norm * at_query, axis=0, keepdims=True)
+
+    for s in range(SLOTS):
+        f_lane = iota((GROUP, 128), 1) - s * Q
+        f_row = iota((GROUP, 128), 0)
+        folds[0, s] = (f_lane == lax.rem(f_row, TALL)).astype(F32).astype(BF16)
+        folds[1, s] = (f_lane == TALL + lax.rem(f_row, SHORT)).astype(F32).astype(BF16)
     take(got, got_sem)
 
     g = got[...].reshape(DEVS, 128)
@@ -432,6 +432,9 @@
     pulled = (mixed_ref[...] * (inv_col * inv_col * tan_col)).astype(BF16)
     gb = -tn(low_half, pulled)
 
+    for j in range(WIDTH // 128):
+        piece_out[0, pl.ds(j * RANK, RANK), :] = ga[:, j * 128 : (j + 1) * 128]
+
     take(wrec, w_sem)
     w = wrec[...].reshape(DEVS, 128)
     lost = jnp.where((lane == LOSS_LANE) & (iota((DEVS, 128), 0) < CHIPS), w, 0.0)
@@ -439,10 +442,10 @@
     push(losses.at[core], losses.at[core], small_sem.at[13], loss_sem, sibling)
     w_t = jnp.transpose(w) * jnp.where(lane1 < CHIPS, 1.0 / flags[0, 0:1, :], 1.0 / flags[1, 0:1, :])
     for s in range(SLOTS):
-        for piece in split(w_t[VOFF + s * RANK : VOFF + (s + 1) * RANK, :], 2):
-            gb = gb + nn(piece, slot_rows(s))
+        v_hi, v_lo = split(w_t[VOFF + s * RANK : VOFF + (s + 1) * RANK, :], 2)
+        r = nn(jnp.concatenate([v_hi, v_lo], axis=0), slot_rows(s))
+        gb = gb + r[0:RANK] + r[RANK : 2 * RANK]
     for j in range(WIDTH // 128):
-        piece_out[0, pl.ds(j * RANK, RANK), :] = ga[:, j * 128 : (j + 1) * 128]
         piece_out[1, pl.ds(j * RANK, RANK), :] = gb[:, j * 128 : (j + 1) * 128]
 
     to_all(lambda chip, c: push(row_of(piece_out, chip * 2 + c), row_of(piece_in, me), small_sem.at[9], rs_sem, (chip * 2 + c, mp)), True)
@@ -527,27 +530,15 @@
     take(cand_out.at[0], small_sem.at[12])
 
 
-def finish(loss_in, pieces_ref, table_in, loss_ref, ga_ref, gb_ref, table_out, buf, in_sem, out_sem):
-    step = ROWS // 4
-    ins = [
-        pltpu.make_async_copy(table_in.at[pl.ds(i * step, step), :], buf.at[pl.ds(i * step, step), :], in_sem.at[i])
-        for i in range(4)
-    ]
-    outs = [
-        pltpu.make_async_copy(buf.at[pl.ds(i * step, step), :], table_out.at[pl.ds(i * step, step), :], out_sem.at[i])
-        for i in range(4)
-    ]
-    for cp in ins:
-        cp.start()
-    loss_ref[...] = loss_in[...]
-    for j in range(WIDTH // 128):
-        ga_ref[:, pl.ds(j * 128, 128)] = pieces_ref[0, pl.ds(j * RANK, RANK), :]
-        gb_ref[:, pl.ds(j * 128, 128)] = pieces_ref[1, pl.ds(j * RANK, RANK), :]
-    for cin, cout in zip(ins, outs, strict=True):
-        cin.wait()
-        cout.start()
-    for cp in outs:
-        cp.wait()
+def finish(loss_in, pieces_ref, table_in, loss_ref, ga_ref, gb_ref, table_out):
+    table_out[...] = table_in[...]
+
+    @pl.when(pl.program_id(0) == 0)
+    def _():
+        loss_ref[...] = loss_in[...]
+        for j in range(WIDTH // 128):
+            ga_ref[:, pl.ds(j * 128, 128)] = pieces_ref[0, pl.ds(j * RANK, RANK), :]
+            gb_ref[:, pl.ds(j * 128, 128)] = pieces_ref[1, pl.ds(j * RANK, RANK), :]
 
 
 def shards(hidden, down, up, passages, ids, storage):
@@ -602,12 +593,17 @@
         compiler_params=pltpu.CompilerParams(collective_id=0, has_side_effects=True, vmem_limit_bytes=56 << 20),
         name="contrastive",
     )(ids.T, hidden, down, up, passages, storage.reshape(ROWS, 128))
+    rows = pl.BlockSpec((ROWS // 2, WIDTH), lambda i: (i, 0))
+
+    def whole(*dims):
+        return pl.BlockSpec(dims, lambda i: (0,) * len(dims))
+
     loss, ga, gb, table = pl.pallas_call(
         finish,
         out_shape=(shape((1, 1), F32), shape((RANK, WIDTH), F32), shape((RANK, WIDTH), F32), shape((ROWS, WIDTH), BF16)),
-        in_specs=[vm, vm, hbm],
-        out_specs=(vm, vm, vm, hbm),
-        scratch_shapes=[pltpu.VMEM((ROWS, WIDTH), BF16), dma((4,)), dma((4,))],
+        grid=(2,),
+        in_specs=[whole(1, 1), whole(2, DEVS, 128), rows],
+        out_specs=(whole(1, 1), whole(RANK, WIDTH), whole(RANK, WIDTH), rows),
         name="finish",
     )(loss, pieces, table)
     return loss.reshape(()), ga, gb, table

time: 84.5 us -> 82.1 us (0.972)
  Pallas kernels: 83.7 us -> 81.3 us
    pallas_call x1, Pallas kernels: 4.14 us -> 2.64 us  [shards(): pl.pallas_call(finish, out_shape=(shape((1, 1), F32), shape((RANK, WIDTH)...]
where the time goes in v4:
time: 82.1 us; the launch traced here: 82 us
  Pallas kernels  81.3 us (99%)
    pallas_call x1, Pallas kernels, shards(): pl.pallas_call(kernel, out_shape=(shape((1, 1), F32), shape((2, DEVS, 128...  78.7 us
    pallas_call x1, Pallas kernels, shards(): pl.pallas_call(finish, out_shape=(shape((1, 1), F32), shape((RANK, WIDTH)...  2.64 us

profile of v4, /device:TPU:1, one launch (start us, length us, event | category | flops | bytes accessed | tf_op | source)
XLA Modules:
  0.0 82.0 jit_solution(5662648001464117319)
XLA Ops:
  0.6 78.7 %contrastive.1 = (f32[1,1]{1,0:T(1,128)}, f32[2,128,128]{2,1,0:T(8,128)}, bf16[384,1024]{1,0:T(8,128)(2,1)}) custom-call(s32[8,24]{1,0:T(8,128)} %bitcast.4, bf16[24,1024]{1,0:T(8,128)(2,1)} %hidden_hbm.1, bf16[16,1024]{1,0:T(8,128)(2,1)} %down_hbm.1, bf16[16,1024]{1,0:T(8,128)(2,1)} %up_hbm.1, bf16[384,1024]{1,0:T(8,128)(2,1)} %pass_hbm.1, s32[384,128]{1,0:T(8,128)} %bitcast.3), custom_call_target="tpu_custom_call" | custom-call | tf_op jit(solution)/shard_map/contrastive/pallas_call | solution.py:548
  79.3 2.6 %finish.1 = (f32[1,1]{1,0:T(1,128)}, f32[16,1024]{1,0:T(8,128)}, f32[16,1024]{1,0:T(8,128)}, bf16[384,1024]{1,0:T(8,128)(2,1)}) custom-call(f32[1,1]{1,0:T(1,128)} %get-tuple-element.11.loss_in, f32[2,128,128]{2,1,0:T(8,128)} %get-tuple-element.12.pieces_ref, bf16[384,1024]{1,0:T(8,128)(2,1)} %get-tuple-element.13.table_in), custom_call_target="tpu_custom_call" | custom-call | tf_op jit(solution)/shard_map/finish/pallas_call | solution.py:601

commit v5 on v4

--- a/solution.py
+++ b/solution.py
@@ -319,41 +319,34 @@
     def far_first(m):
         return ((8 - m) // 2) * (1 if m % 2 else -1)
 
+    def hops(o):
+        return min(o % NY, NY - o % NY)
+
+    paths = sorted(((dy, dz) for dy in range(NY) for dz in range(NZ)), key=lambda w: -hops(w[0]) - hops(w[1]))
+
     def to_all(send, both):
-        inner = [lax.rem(z + far_first(n) + NZ, NZ) for n in range(NZ)]
-        cores = (1 - core, core) if both else (core,)
-
-        def far_rows(m, carry):
-            base = lax.rem(y + swing(m) + NY, NY) * NZ
-            for n in inner:
-                for c in cores:
-                    send(base + n, c)
-            return carry
-
-        lax.fori_loop(0, NY - 1, far_rows, 0)
-        for i, n in enumerate(inner):
-            for c in cores[: len(cores) if i < NZ - 1 else len(cores) - 1]:
-                send(y * NZ + n, c)
+        rows_y = [lax.rem(y + o, NY) * NZ for o in range(NY)]
+        cols_z = [lax.rem(z + o, NZ) for o in range(NZ)]
+        for dy, dz in paths:
+            for c in (1 - core, core) if both else (core,):
+                if dy + dz > 0 or (both and c is not core):
+                    send(rows_y[dy] + cols_z[dz], c)
 
     def row_of(ref, chip):
         return ref.at[:, pl.ds(chip, 1), :]
 
     home = (chip_me // quarter) == mp
-    others = [lax.rem(mp + dk, NX) for dk in (2, 1, 3)]
-
-    def give(m, c):
-        first = lax.rem(z + swing(m) + NZ, NZ)
-        for j in (first, first + NZ):
+    ways = sorted(((dz, dk) for dz in range(NZ) for dk in range(NX)), key=lambda w: -hops(w[0]) - min(w[1], NX - w[1]))
+    for dz, dk in ways:
+        for dy in (0, 1):
+            j = dy * NZ + lax.rem(z + dz, NZ)
             chip = mp * quarter + j
-            for k in others:
-                push(row_of(summed, j), row_of(got, chip_me), small_sem.at[7], got_sem, (chip * 2 + core, k))
-
-            @pl.when(chip != chip_me)
-            def _():
-                push(row_of(summed, j), row_of(got, chip_me), small_sem.at[7], got_sem, (chip * 2 + core, mp))
-        return c
-
-    lax.fori_loop(0, NZ, give, 0)
+            if dz + dk > 0:
+                push(row_of(summed, j), row_of(got, chip_me), small_sem.at[7], got_sem, (chip * 2 + core, lax.rem(mp + dk, NX)))
+            else:
+                @pl.when(chip != chip_me)
+                def _():
+                    push(row_of(summed, j), row_of(got, chip_me), small_sem.at[7], got_sem, (chip * 2 + core, mp))
 
     @pl.when(home)
     def _():

time: 82.1 us -> 81.7 us (level)
  no operation moved by 1% of the time
where the time goes in v5:
time: 81.7 us; the launch traced here: 81.5 us
  Pallas kernels  80.9 us (99%)
    pallas_call x1, Pallas kernels, shards(): pl.pallas_call(kernel, out_shape=(shape((1, 1), F32), shape((2, DEVS, 128...  78.3 us
    pallas_call x1, Pallas kernels, shards(): pl.pallas_call(finish, out_shape=(shape((1, 1), F32), shape((RANK, WIDTH)...  2.64 us

profile of v5, /device:TPU:1, one launch (start us, length us, event | category | flops | bytes accessed | tf_op | source)
XLA Modules:
  0.0 81.5 jit_solution(17935860901022390232)
XLA Ops:
  0.6 78.3 %contrastive.1 = (f32[1,1]{1,0:T(1,128)}, f32[2,128,128]{2,1,0:T(8,128)}, bf16[384,1024]{1,0:T(8,128)(2,1)}) custom-call(s32[8,24]{1,0:T(8,128)} %bitcast.4, bf16[24,1024]{1,0:T(8,128)(2,1)} %hidden_hbm.1, bf16[16,1024]{1,0:T(8,128)(2,1)} %down_hbm.1, bf16[16,1024]{1,0:T(8,128)(2,1)} %up_hbm.1, bf16[384,1024]{1,0:T(8,128)(2,1)} %pass_hbm.1, s32[384,128]{1,0:T(8,128)} %bitcast.3), custom_call_target="tpu_custom_call" | custom-call | tf_op jit(solution)/shard_map/contrastive/pallas_call | solution.py:541
  78.9 2.6 %finish.1 = (f32[1,1]{1,0:T(1,128)}, f32[16,1024]{1,0:T(8,128)}, f32[16,1024]{1,0:T(8,128)}, bf16[384,1024]{1,0:T(8,128)(2,1)}) custom-call(f32[1,1]{1,0:T(1,128)} %get-tuple-element.11.loss_in, f32[2,128,128]{2,1,0:T(8,128)} %get-tuple-element.12.pieces_ref, bf16[384,1024]{1,0:T(8,128)(2,1)} %get-tuple-element.13.table_in), custom_call_target="tpu_custom_call" | custom-call | tf_op jit(solution)/shard_map/finish/pallas_call | solution.py:594
